TPU v7x, 32 devices: a whole 2x2x4 slice. The times are simulated.
32 devices in a mesh: groups: 2 (over x), tiles: 16 (over z, y, core).
Axes of the slice: x: 2, y: 2, z: 4, core: 2. Of those that a mesh axis runs over, the one named last changes fastest.
Arguments:
- obs_position: float32 [2, 65536], P(None, ('groups', 'tiles')), parts along dimension 1, may hold values from 0 to 24, as said below
- obs_sd: float32 [65536], P(('groups', 'tiles')), parts along dimension 0, may hold values from 0.5 to 2
- obs_var: float32 [65536], P(('groups', 'tiles')), parts along dimension 0, may hold values from 0.5 to 2
- innovations: float32 [8, 65536], P(None, ('groups', 'tiles')), parts along dimension 1, may hold values from -12 to 12
- obs_target: int32 [65536], P(('groups', 'tiles')), parts along dimension 0, may hold values from 0 to 32767, as said below
- pair_table: int32 [32, 4, 2], P(('groups', 'tiles')), parts along dimension 0, may hold values from 0 to 15, as said below
- pair_count: int32 [32], P(('groups', 'tiles')), parts along dimension 0, may hold values from 1 to 4, as said below
Outputs:
- solution_field: float32 [8, 65536], P(None, ('groups', 'tiles')), parts along dimension 1
- residual: float32 [8, 65536], P(None, ('groups', 'tiles')), parts along dimension 1
There are 2 independent parts, one for each index of `groups`. A program takes and returns all parts, laid end to end along the dimension named above; each array names one. Nothing has to cross between parts.
Inputs may be any that keep to these rules, and one draw needn't show every extreme that they name: A permutation; the tile of an observation is obs_target // 2048; of the rows of one device at most 192 go to any one tile, and exactly 192 to some tile. `pair_table`: row d holds (d, d), (d, d + 1), ..., (d, d + pair_count[d] - 1) in its first slots and (d, d) in the others; blocks of pairs that are not listed are zero. `pair_count`: equals 4 on some row. `obs_position`: the first coordinates of tile t lie between bounds of their own that rise with t; the second coordinate lies in 0 to 8.
All inputs are finite; a program needn't handle non-finite values.
Results may differ from a plain program's by a relative error of at most 0.0003.
Values sent between devices are 32-bit elements; how exact they have to be, the bound alone decides.
No kernel may reach another device: no remote copies, remote signals or barrier semaphores. Data moves between devices by JAX's collectives and lax.ppermute only.
A program may use at most 64 MiB of HBM per device.

v0:
```python
import jax
import jax.numpy as jnp
from jax import lax
from jax.sharding import PartitionSpec as P

ITERS = 2


def shifted(value, axis, by):
    length = lax.axis_size(axis)
    pairs = [(i, i + by) for i in range(length) if 0 <= i + by < length]
    return lax.ppermute(value, axis, pairs)


def wendland_block(row_geo, col_geo):
    delta_x = row_geo[0][:, None] - col_geo[0][None, :]
    delta_y = row_geo[1][:, None] - col_geo[1][None, :]
    distance = jnp.sqrt(delta_x * delta_x + delta_y * delta_y)
    inside = jnp.maximum(1.0 - distance, 0.0)
    squared = inside * inside
    return squared * squared * (4.0 * distance + 1.0) * row_geo[2][:, None] * col_geo[2][None, :]


def pair_part(geo_rows, dir_rows, geo_cols, dir_cols, first_block, block_count):
    block_rows = min(128, geo_rows.shape[1])

    def one_block(counter, totals):
        into_rows, into_cols = totals
        row_start = (first_block + counter) * block_rows
        row_geo = lax.dynamic_slice_in_dim(geo_rows, row_start, block_rows, 1)
        block_corr = wendland_block(row_geo, geo_cols)
        from_cols = lax.dot_general(
            dir_cols,
            block_corr,
            (((1,), (1,)), ((), ())),
            precision=lax.Precision.HIGHEST,
            preferred_element_type=jnp.float32,
        )
        picked = lax.dynamic_slice_in_dim(dir_rows, row_start, block_rows, 1)
        from_rows = jnp.dot(
            picked, block_corr, precision=lax.Precision.HIGHEST, preferred_element_type=jnp.float32
        )
        current = lax.dynamic_slice_in_dim(into_rows, row_start, block_rows, 1)
        into_rows = lax.dynamic_update_slice_in_dim(into_rows, current + from_cols, row_start, 1)
        return (into_rows, into_cols + from_rows)

    blank_dir = jnp.zeros_like(dir_rows)
    return lax.fori_loop(0, block_count, one_block, (blank_dir, blank_dir))


def fetch_right(value, neighbours):
    return [shifted(value, "tiles", -hop_size) for hop_size in range(1, neighbours + 1)]


def send_up(outgoing):
    arrived = jnp.zeros_like(outgoing[0])
    for hop_size in range(1, outgoing.shape[0]):
        arrived = arrived + shifted(outgoing[hop_size], "tiles", hop_size)
    return arrived


def own_pairs(direction, variance, geometry, near_geo, near_dir, pair_table, pair_total, my_tile):
    stack_geo = jnp.stack([geometry] + near_geo)
    stack_dir = jnp.stack([direction] + near_dir)
    all_blocks = geometry.shape[1] // min(128, geometry.shape[1])
    result = variance[None, :] * direction
    outgoing = jnp.zeros(stack_dir.shape, jnp.float32)
    for slot_index in range(pair_table.shape[1]):
        pair_offset = pair_table[0, slot_index, 1] - my_tile

        def compute_pair(offset_now):
            return pair_part(
                geometry, direction, stack_geo[offset_now], stack_dir[offset_now], 0, all_blocks
            )

        def skip_pair(offset_now):
            blank_dir = jnp.zeros_like(direction)
            return (blank_dir, blank_dir)

        into_own, into_other = lax.cond(
            slot_index < pair_total, compute_pair, skip_pair, pair_offset
        )
        result = result + into_own
        outgoing = outgoing.at[pair_offset].add(jnp.where(pair_offset > 0, into_other, 0.0))
    return (result, outgoing)


def squares(residual):
    return lax.psum(jnp.sum(residual * residual, axis=1), "tiles")


def local(obs_position, obs_sd, obs_var, innovations, obs_target, pair_table, pair_count):
    tile_count = lax.axis_size("tiles")
    my_tile = lax.axis_index("tiles")
    tile_rows = obs_sd.shape[0]
    capacity = 3 * tile_rows // (2 * tile_count)
    owner = obs_target // tile_rows
    place_slot = obs_target % tile_rows
    one_hot = (owner[:, None] == jnp.arange(tile_count, dtype=jnp.int32)[None, :]).astype(jnp.int32)
    earlier = jnp.cumsum(one_hot, axis=0) - one_hot
    rank_in = jnp.sum(earlier * one_hot, axis=1)
    column = owner * capacity + rank_in
    fields = jnp.concatenate(
        [
            obs_position,
            obs_sd[None, :],
            obs_var[None, :],
            innovations,
            (place_slot + 1).astype(jnp.float32)[None, :],
        ],
        axis=0,
    )
    outbox = (
        jnp.zeros((fields.shape[0], tile_count * capacity), jnp.float32).at[:, column].set(fields)
    )
    inbox = lax.all_to_all(outbox, "tiles", split_axis=1, concat_axis=1, tiled=True)
    landed = inbox[-1].astype(jnp.int32) - 1
    target_col = jnp.where(landed >= 0, landed, tile_rows)
    arrived = (
        jnp.zeros((fields.shape[0] - 1, tile_rows), jnp.float32)
        .at[:, target_col]
        .set(inbox[:-1], mode="drop")
    )
    geometry = arrived[0:3]
    variance = arrived[3]
    right_side = arrived[4:]
    neighbours = pair_table.shape[1] - 1
    pair_total = pair_count[0]
    right_geo = [shifted(geometry, "tiles", -hop_size) for hop_size in range(1, neighbours + 1)]
    solution_field = jnp.zeros_like(right_side)
    residual = right_side
    direction = right_side
    norm_now = squares(residual)
    for iteration in range(ITERS):
        right_dir = fetch_right(direction, neighbours)
        image, outgoing = own_pairs(
            direction, variance, geometry, right_geo, right_dir, pair_table, pair_total, my_tile
        )
        image = image + send_up(outgoing)
        alpha = norm_now / lax.psum(jnp.sum(direction * image, axis=1), "tiles")
        solution_field = solution_field + alpha[:, None] * direction
        residual = residual - alpha[:, None] * image
        if iteration + 1 < ITERS:
            norm_next = squares(residual)
            direction = residual + (norm_next / norm_now)[:, None] * direction
            norm_now = norm_next
    return (solution_field, residual)


def solution(mesh):
    placed = (
        P(None, ("groups", "tiles")),
        P(("groups", "tiles")),
        P(("groups", "tiles")),
        P(None, ("groups", "tiles")),
        P(("groups", "tiles")),
        P(("groups", "tiles"), None, None),
        P(("groups", "tiles")),
    )
    return jax.shard_map(
        local,
        mesh=mesh,
        in_specs=placed,
        out_specs=(P(None, ("groups", "tiles")), P(None, ("groups", "tiles"))),
        check_vma=False,
    )
```

profile of v0, /device:TPU:0, one launch (start us, length us, event | category | flops | bytes accessed | tf_op | source)
XLA Modules:
  0.0 949.6 jit_solution(10894059457788872141)
XLA Ops:
  1.4 4.5 reduce-window.6
  8.9 6.0 scatter_custom_fusion
  16.2 7.4 all-to-all-start
  27.0 6.7 all-to-all-done
  35.7 8.7 scatter_custom_fusion.1
  57.6 4.4 collective-permute-done.4
  66.2 93.4 %conditional.10 = (f32[8,2048]{1,0:T(8,128)}, f32[8,2048]{1,0:T(8,128)}) conditional(s32[]{:T(128)} %bitcast.37, () %tuple.220, (s32[]{:T(128)}, f32[4,3,2048]{2,0,1:T(4,128)S(1)}, f32[4,8,2048]{2,1,0:T(8,128)S(1)}, f32[3,2048]{0,1:T(8,128)S(1)}, f32[8,2048]{1,0:T(8,128)S(1)}) %tuple.221), branch_computations={%region_15.16_spmd, %region_16.19_spmd} | conditional | flops 57705480 | bytes 808271 | solution.py:80
  67.3 92.3 %while.130 = (s32[]{:T(128)}, f32[8,2048]{1,0:T(8,128)}, f32[8,2048]{1,0:T(8,128)}, f32[3,2048]{1,0:T(4,128)S(1)}, f32[3,2048]{1,0:T(4,128)S(1)}, /*index=5*/f32...) while((s32[]{:T(128)}, f32[8,2048]{1,0:T(8,128)}, ...), condition=%wide.region_18.18_spmd.clone, body=%wide.region_17.17_spmd.clone.sunk | while | flops 57705476 | bytes 316593 | solution.py:48
  110.1 2.9 fusion.316
  159.5 93.4 %conditional.9 = (f32[8,2048]{1,0:T(8,128)}, f32[8,2048]{1,0:T(8,128)}) conditional(s32[]{:T(128)} %bitcast.35, () %tuple.218, (s32[]{:T(128)}, f32[4,3,2048]{2,0,1:T(4,128)S(1)}, f32[4,8,2048]{2,1,0:T(8,128)S(1)}, f32[3,2048]{0,1:T(8,128)S(1)}, f32[8,2048]{1,0:T(8,128)S(1)}) %tuple.219), branch_computations={%region_11.12_spmd, %region_12.15_spmd} | conditional | flops 57705480 | bytes 808271 | solution.py:80
  160.6 92.3 %while.129 = (s32[]{:T(128)}, f32[8,2048]{1,0:T(8,128)}, f32[8,2048]{1,0:T(8,128)}, f32[3,2048]{1,0:T(4,128)S(1)}, f32[3,2048]{1,0:T(4,128)S(1)}, /*index=5*/f32...) while((s32[]{:T(128)}, f32[8,2048]{1,0:T(8,128)}, ...), condition=%wide.region_14.14_spmd.clone, body=%wide.region_13.13_spmd.clone.sunk | while | flops 57705476 | bytes 316593 | solution.py:48
  174.3 2.9 fusion.320
  209.3 2.9 fusion.320
  252.9 93.6 %conditional.8 = (f32[8,2048]{1,0:T(8,128)}, f32[8,2048]{1,0:T(8,128)}) conditional(s32[]{:T(128)} %bitcast.25, () %tuple.216, (s32[]{:T(128)}, f32[4,3,2048]{2,0,1:T(4,128)S(1)}, f32[4,8,2048]{2,1,0:T(8,128)S(1)}, f32[3,2048]{0,1:T(8,128)S(1)}, f32[8,2048]{1,0:T(8,128)S(1)}) %tuple.217), branch_computations={%region_7.8_spmd, %region_8.11_spmd} | conditional | flops 57705480 | bytes 808271 | solution.py:80
  254.1 92.5 %while.128 = (s32[]{:T(128)}, f32[8,2048]{1,0:T(8,128)}, f32[8,2048]{1,0:T(8,128)}, f32[3,2048]{1,0:T(4,128)S(1)}, f32[3,2048]{1,0:T(4,128)S(1)}, /*index=5*/f32...) while((s32[]{:T(128)}, f32[8,2048]{1,0:T(8,128)}, ...), condition=%wide.region_10.10_spmd.clone, body=%wide.region_9.9_spmd.clone.sunk | while | flops 57705476 | bytes 316593 | solution.py:48
  256.1 2.9 fusion.324
  261.9 2.9 fusion.324
  267.8 2.9 fusion.324
  273.6 2.9 fusion.324
  279.4 2.9 fusion.324
  285.3 2.9 fusion.324
  291.1 2.9 fusion.324
  296.9 2.9 fusion.324
  302.8 2.9 fusion.324
  308.6 2.9 fusion.324
  314.4 2.9 fusion.324
  320.2 2.9 fusion.324
  326.1 2.9 fusion.324
  331.9 2.9 fusion.324
  337.7 2.9 fusion.324
  343.6 2.9 fusion.324
  353.5 100.3 %collective-permute-start.8 = (f32[8,2048]{1,0:T(8,128)S(1)}, f32[8,2048]{1,0:T(8,128)S(1)}, u32[]{:S(2)}, u32[]{:S(2)}) collective-permute-start(f32[8,2048]{1,0:T(8,128)S(1)} %get-tuple-element.1827), channel_id=1, source_target_pairs={{0,3},{1,4},{2,5},{3,6},{4,7},{5,8},{6,9},{7,10},{8,11},{9,12},{10... | collective-permute-start | bytes 196616 | tf_op jit(solution)/shard_map/ppermute | solution.py:12
  456.9 31.3 %all-reduce = (f32[8]{0:T(128)S(1)}, f32[8]{0:T(128)S(1)}) all-reduce(f32[8]{0:T(128)S(1)} %get-tuple-element.1651, f32[8]{0:T(128)S(1)} %get-tuple-element.1650), channel_id=1, replica_groups=mesh['groups'=2,'tiles'=16] {'tiles'}, use_global_device_ids=true, to_apply=%region_6.7 | all-reduce | flops 16 | bytes 128 | tf_op jit(solution)/shard_map/psum | solution.py:89
  488.4 29.5 %psum.30 = f32[8]{0:T(128)S(1)} all-reduce(f32[8]{0:T(128)S(1)} %multiply_reduce_fusion.1), channel_id=1, replica_groups=mesh['groups'=2,'tiles'=16] {'tiles'}, use_global_device_ids=true, to_apply=%region_30.31 | all-reduce | flops 8 | bytes 64 | tf_op jit(solution)/shard_map/psum | solution.py:89
  521.9 4.3 collective-permute-done.10
  528.9 93.4 %conditional.14 = (f32[8,2048]{1,0:T(8,128)}, f32[8,2048]{1,0:T(8,128)}) conditional(s32[]{:T(128)} %bitcast.37, () %tuple.228, (s32[]{:T(128)}, f32[4,3,2048]{2,0,1:T(4,128)S(1)}, f32[4,8,2048]{2,1,0:T(8,128)S(1)}, f32[3,2048]{0,1:T(8,128)S(1)}, f32[8,2048]{1,0:T(8,128)S(1)}) %tuple.229), branch_computations={%region_39.40_spmd, %region_40.43_spmd} | conditional | flops 57705480 | bytes 808271 | solution.py:80
  530.0 92.3 %while.134 = (s32[]{:T(128)}, f32[8,2048]{1,0:T(8,128)}, f32[8,2048]{1,0:T(8,128)}, f32[3,2048]{1,0:T(4,128)S(1)}, f32[3,2048]{1,0:T(4,128)S(1)}, /*index=5*/f32...) while((s32[]{:T(128)}, f32[8,2048]{1,0:T(8,128)}, ...), condition=%wide.region_42.42_spmd.clone, body=%wide.region_41.41_spmd.clone.sunk | while | flops 57705476 | bytes 316593 | solution.py:48
  572.7 2.9 fusion.300
  622.2 93.4 %conditional.13 = (f32[8,2048]{1,0:T(8,128)}, f32[8,2048]{1,0:T(8,128)}) conditional(s32[]{:T(128)} %bitcast.35, () %tuple.226, (s32[]{:T(128)}, f32[4,3,2048]{2,0,1:T(4,128)S(1)}, f32[4,8,2048]{2,1,0:T(8,128)S(1)}, f32[3,2048]{0,1:T(8,128)S(1)}, f32[8,2048]{1,0:T(8,128)S(1)}) %tuple.227), branch_computations={%region_35.36_spmd, %region_36.39_spmd} | conditional | flops 57705480 | bytes 808271 | solution.py:80
  623.3 92.3 %while.133 = (s32[]{:T(128)}, f32[8,2048]{1,0:T(8,128)}, f32[8,2048]{1,0:T(8,128)}, f32[3,2048]{1,0:T(4,128)S(1)}, f32[3,2048]{1,0:T(4,128)S(1)}, /*index=5*/f32...) while((s32[]{:T(128)}, f32[8,2048]{1,0:T(8,128)}, ...), condition=%wide.region_38.38_spmd.clone, body=%wide.region_37.37_spmd.clone.sunk | while | flops 57705476 | bytes 316593 | solution.py:48
  637.0 2.9 fusion.304
  671.9 2.9 fusion.304
  715.6 93.6 %conditional.12 = (f32[8,2048]{1,0:T(8,128)}, f32[8,2048]{1,0:T(8,128)}) conditional(s32[]{:T(128)} %bitcast.25, () %tuple.224, (s32[]{:T(128)}, f32[4,3,2048]{2,0,1:T(4,128)S(1)}, f32[4,8,2048]{2,1,0:T(8,128)S(1)}, f32[3,2048]{0,1:T(8,128)S(1)}, f32[8,2048]{1,0:T(8,128)S(1)}) %tuple.225), branch_computations={%region_31.32_spmd, %region_32.35_spmd} | conditional | flops 57705480 | bytes 808271 | solution.py:80
  716.7 92.5 %while.132 = (s32[]{:T(128)}, f32[8,2048]{1,0:T(8,128)}, f32[8,2048]{1,0:T(8,128)}, f32[3,2048]{1,0:T(4,128)S(1)}, f32[3,2048]{1,0:T(4,128)S(1)}, /*index=5*/f32...) while((s32[]{:T(128)}, f32[8,2048]{1,0:T(8,128)}, ...), condition=%wide.region_34.34_spmd.clone, body=%wide.region_33.33_spmd.clone.sunk | while | flops 57705476 | bytes 316593 | solution.py:48
  718.8 2.9 fusion.308
  724.6 2.9 fusion.308
  816.2 100.2 %collective-permute-start.14 = (f32[8,2048]{1,0:T(8,128)S(1)}, f32[8,2048]{1,0:T(8,128)S(1)}, u32[]{:S(2)}, u32[]{:S(2)}) collective-permute-start(f32[8,2048]{1,0:T(8,128)S(1)} %get-tuple-element.1824), channel_id=1, source_target_pairs={{0,3},{1,4},{2,5},{3,6},{4,7},{5,8},{6,9},{7,10},{8,11},{9,12},{10... | collective-permute-start | bytes 196616 | tf_op jit(solution)/shard_map/ppermute | solution.py:12
  919.4 29.5 %psum.31 = f32[8]{0:T(128)S(1)} all-reduce(f32[8]{0:T(128)S(1)} %get-tuple-element.1770), channel_id=1, replica_groups=mesh['groups'=2,'tiles'=16] {'tiles'}, use_global_device_ids=true, to_apply=%region_48.49 | all-reduce | flops 8 | bytes 64 | tf_op jit(solution)/shard_map/psum | solution.py:140
  (578 shorter events, 543.2 us)
Async XLA Ops:
  14.8 8.7 copy-start
  16.2 17.4 %all-to-all-start = ((f32[13,16,192]{2,0,1:T(8,128)}), f32[13,16,192]{2,0,1:T(8,128)S(1)}, u32[]{:S(2)}, u32[]{:S(2)}) async-start(f32[13,16,192]{2,0,1:T(8,128)} %copy.226), calls=%async_computation | async-start | bytes 524288 | tf_op jit(solution)/shard_map/all_to_all | solution.py:116
  44.4 4.4 copy-start.1
  44.9 11.2 %collective-permute-start = (f32[3,2048]{1,0:T(4,128)S(1)}, f32[3,2048]{1,0:T(4,128)S(1)}, u32[]{:S(2)}, u32[]{:S(2)}) collective-permute-start(f32[3,2048]{1,0:T(4,128)S(1)} %copy.230), channel_id=1, source_target_pairs={{1,0},{2,1},{3,2},{4,3},{5,4},{6,5},{7,6},{8,7},{9,8},{10,9},{11,1... | collective-permute-start | bytes 73736 | tf_op jit(solution)/shard_map/ppermute | solution.py:12
  46.2 11.2 %collective-permute-start.1 = (f32[3,2048]{1,0:T(4,128)S(1)}, f32[3,2048]{1,0:T(4,128)S(1)}, u32[]{:S(2)}, u32[]{:S(2)}) collective-permute-start(f32[3,2048]{1,0:T(4,128)S(1)} %copy.230), channel_id=1, source_target_pairs={{2,0},{3,1},{4,2},{5,3},{6,4},{7,5},{8,6},{9,7},{10,8},{11,9},{12,... | collective-permute-start | bytes 73736 | tf_op jit(solution)/shard_map/ppermute | solution.py:12
  47.5 9.9 %collective-permute-start.2 = (f32[3,2048]{1,0:T(4,128)S(1)}, f32[3,2048]{1,0:T(4,128)S(1)}, u32[]{:S(2)}, u32[]{:S(2)}) collective-permute-start(f32[3,2048]{1,0:T(4,128)S(1)} %copy.230), channel_id=1, source_target_pairs={{3,0},{4,1},{5,2},{6,3},{7,4},{8,5},{9,6},{10,7},{11,8},{12,9},{13... | collective-permute-start | bytes 73736 | tf_op jit(solution)/shard_map/ppermute | solution.py:12
  53.1 4.5 collective-permute-start.3
  54.4 7.6 collective-permute-start.4
  56.1 8.8 collective-permute-start.5
  350.9 103.6 %collective-permute-start.6 = (f32[8,2048]{1,0:T(8,128)S(1)}, f32[8,2048]{1,0:T(8,128)S(1)}, u32[]{:S(2)}, u32[]{:S(2)}) collective-permute-start(f32[8,2048]{1,0:T(8,128)S(1)} %get-tuple-element.1828), channel_id=1, source_target_pairs={{0,1},{1,2},{2,3},{3,4},{4,5},{5,6},{6,7},{7,8},{8,9},{9,10},{10,1... | collective-permute-start | bytes 196616 | tf_op jit(solution)/shard_map/ppermute | solution.py:12
  352.2 102.3 %collective-permute-start.7 = (f32[8,2048]{1,0:T(8,128)S(1)}, f32[8,2048]{1,0:T(8,128)S(1)}, u32[]{:S(2)}, u32[]{:S(2)}) collective-permute-start(f32[8,2048]{1,0:T(8,128)S(1)} %get-tuple-element.1826), channel_id=1, source_target_pairs={{0,2},{1,3},{2,4},{3,5},{4,6},{5,7},{6,8},{7,9},{8,10},{9,11},{10,... | collective-permute-start | bytes 196616 | tf_op jit(solution)/shard_map/ppermute | solution.py:12
  353.5 102.2 %collective-permute-start.8 = (f32[8,2048]{1,0:T(8,128)S(1)}, f32[8,2048]{1,0:T(8,128)S(1)}, u32[]{:S(2)}, u32[]{:S(2)}) collective-permute-start(f32[8,2048]{1,0:T(8,128)S(1)} %get-tuple-element.1827), channel_id=1, source_target_pairs={{0,3},{1,4},{2,5},{3,6},{4,7},{5,8},{6,9},{7,10},{8,11},{9,12},{10... | collective-permute-start | bytes 196616 | tf_op jit(solution)/shard_map/ppermute | solution.py:12
  518.0 3.9 collective-permute-start.9
  519.3 6.9 collective-permute-start.10
  520.6 6.9 collective-permute-start.11
  813.6 102.8 %collective-permute-start.12 = (f32[8,2048]{1,0:T(8,128)S(1)}, f32[8,2048]{1,0:T(8,128)S(1)}, u32[]{:S(2)}, u32[]{:S(2)}) collective-permute-start(f32[8,2048]{1,0:T(8,128)S(1)} %get-tuple-element.1825), channel_id=1, source_target_pairs={{0,1},{1,2},{2,3},{3,4},{4,5},{5,6},{6,7},{7,8},{8,9},{9,10},{10,1... | collective-permute-start | bytes 196616 | tf_op jit(solution)/shard_map/ppermute | solution.py:12
  814.9 101.5 %collective-permute-start.13 = (f32[8,2048]{1,0:T(8,128)S(1)}, f32[8,2048]{1,0:T(8,128)S(1)}, u32[]{:S(2)}, u32[]{:S(2)}) collective-permute-start(f32[8,2048]{1,0:T(8,128)S(1)} %get-tuple-element.1823), channel_id=1, source_target_pairs={{0,2},{1,3},{2,4},{3,5},{4,6},{5,7},{6,8},{7,9},{8,10},{9,11},{10,... | collective-permute-start | bytes 196616 | tf_op jit(solution)/shard_map/ppermute | solution.py:12
  816.2 102.1 %collective-permute-start.14 = (f32[8,2048]{1,0:T(8,128)S(1)}, f32[8,2048]{1,0:T(8,128)S(1)}, u32[]{:S(2)}, u32[]{:S(2)}) collective-permute-start(f32[8,2048]{1,0:T(8,128)S(1)} %get-tuple-element.1824), channel_id=1, source_target_pairs={{0,3},{1,4},{2,5},{3,6},{4,7},{5,8},{6,9},{7,10},{8,11},{9,12},{10... | collective-permute-start | bytes 196616 | tf_op jit(solution)/shard_map/ppermute | solution.py:12
where the time goes:
time: 961 us; the launch traced here: 950 us
  matrix products  551 us (57%)
  starting transfers between devices  225 us (23%)
  blocking collectives  90.3 us (9%)
  local copies, waits for them, and re-layouts  37.1 us (4%)
  waiting for transfers between devices  22.7 us (2%)
  other arithmetic  18.6 us (2%)
    dot_general x96, matrix products, one_block(): lax.dot_general(dir_cols, block_corr, (((1,), (1,)), ((), ())), precision...  281 us
    dot_general x96, matrix products, one_block(): jnp.dot(picked, block_corr, precision=lax.Precision.HIGHEST, preferred_el...  269 us
    ppermute x15, starting transfers between devices, shifted(): return lax.ppermute(value, axis, pairs)  217 us
    psum x2, blocking collectives, squares(): return lax.psum(jnp.sum(residual * residual, axis=1), 'tiles')  60.8 us
    psum x1, blocking collectives, local(): alpha = norm_now / lax.psum(jnp.sum(direction * image, axis=1), 'tiles')  29.5 us
  transfers between devices with their start and end apart: 16, of which 7 were waited for; matrix products, arithmetic and copies ran while one was open for 1% of the time, Pallas kernels for 0%

commit v1 on v0

v1 whole, which is shorter than its diff:
```python
import functools

import jax
import jax.numpy as jnp
from jax import lax
from jax.experimental import pallas as pl
from jax.experimental.pallas import tpu as pltpu
from jax.sharding import PartitionSpec as P

f32, bf16, i32 = jnp.float32, jnp.bfloat16, jnp.int32
LANES = 128
FIELDS = 16
BINS = 128
BATCH = 4
TRANSPOSED = (((1,), (1,)), ((), ()))
VMEM = pl.BlockSpec(memory_space=pltpu.VMEM)
SMEM = pl.BlockSpec(memory_space=pltpu.SMEM)
LIMIT = 40 * 2**20


def iota(shape, axis):
    return lax.broadcasted_iota(i32, shape, axis)


def running_sum_weights():
    shape = (LANES, 2 * LANES)
    row, col = iota(shape, 0), iota(shape, 1)
    return jnp.where((row <= col) | (col >= LANES), 1.0, 0.0).astype(bf16)


def dot(a, b):
    return jnp.dot(a, b, preferred_element_type=f32)


def dot_t(a, b):
    return lax.dot_general(a, b, TRANSPOSED, preferred_element_type=f32)


def invert(places, count):
    chunk_rows, lane_rows, here_rows, low_rows = [], [], [], []
    for chunk, place in enumerate(places):
        high = jnp.right_shift(place, 7)
        here = jnp.where(high == iota((count, LANES), 0), 1.0, 0.0)
        here_rows.append(here.astype(bf16))
        chunk_rows.append((here * float(chunk)).astype(bf16))
        lane_rows.append((here * iota((count, LANES), 1).astype(f32)).astype(bf16))
        low = jnp.bitwise_and(place, LANES - 1)
        low_rows.append(jnp.where(low == iota((LANES, LANES), 0), 1.0, 0.0).astype(bf16))
    left = jnp.concatenate(
        [jnp.concatenate(rows, axis=1) for rows in (chunk_rows, lane_rows, here_rows)], axis=0
    )
    found = dot_t(left, jnp.concatenate(low_rows, axis=1))
    chunk = found[:count].astype(i32)
    lane = found[count : 2 * count].astype(i32)
    return chunk, lane, found[2 * count :] > 0.5


def pick(load, sources, chunk, lane, here):
    total = None
    for source in range(sources):
        value = load(source)
        index = jnp.broadcast_to(lane, value.shape)
        value = jnp.take_along_axis(value, index, axis=1)
        total = value if total is None else jnp.where(chunk == source, value, total)
    return jnp.where(here, total, 0.0)


def outbox_kernel(
    tiles, width, pos_ref, sd_ref, var_ref, innov_ref, target_ref, out_ref, fields, inv_chunk, inv_lane, inv_here
):
    rows = pos_ref.shape[1]
    chunks = rows // LANES
    fields[...] = jnp.zeros_like(fields)
    fields[0:2, :] = pos_ref[...]
    fields[2:3, :] = sd_ref[...]
    fields[3:4, :] = var_ref[...]
    target = target_ref[...]
    owner = target // rows
    fields[12:13, :] = (target - owner * rows + 1).astype(f32)
    fields[4:12, :] = innov_ref[...]
    mine = [
        jnp.where(owner[:, c * LANES : (c + 1) * LANES] == iota((tiles, LANES), 0), 1.0, 0.0)
        for c in range(chunks)
    ]
    sums = dot(jnp.concatenate([m.astype(bf16) for m in mine], axis=0), running_sum_weights())
    before = (iota((tiles, LANES), 0) * width - 1).astype(f32)
    places = []
    for c in range(chunks):
        part = sums[c * tiles : (c + 1) * tiles]
        place = jnp.sum(mine[c] * (part[:, :LANES] + before), axis=0, keepdims=True)
        places.append(place.astype(i32))
        before = before + part[:, LANES:]
    count = tiles * width // LANES
    chunk, lane, here = invert(places, count)
    inv_chunk[...] = chunk
    inv_lane[...] = lane
    inv_here[...] = jnp.where(here, 1, 0)
    per_tile = width // LANES
    for d in range(count):
        out_ref[d // per_tile, :, (d % per_tile) * LANES : (d % per_tile + 1) * LANES] = pick(
            lambda s: fields[:, s * LANES : (s + 1) * LANES],
            chunks,
            inv_chunk[d : d + 1, :],
            inv_lane[d : d + 1, :],
            inv_here[d : d + 1, :] > 0,
        )


def sort_kernel(in_ref, count_ref, share_ref, own_ref, inv_chunk, inv_lane, rank_scr):
    tiles, _, width = in_ref.shape
    rows = own_ref.shape[1]
    chunks = rows // LANES
    per_tile = width // LANES
    sources = tiles * per_tile

    def load(s):
        return in_ref[s // per_tile, :, (s % per_tile) * LANES : (s % per_tile + 1) * LANES]

    weights = running_sum_weights()
    before = jnp.full((BINS, LANES), -1.0, f32)
    for s in range(sources):
        data = load(s)
        bins = jnp.clip((data[1:2] * (BINS / 8.0)).astype(i32), 0, BINS - 1)
        bins = jnp.where(data[12:13] > 0.5, bins, -1)
        member = jnp.where(bins == iota((BINS, LANES), 0), 1.0, 0.0)
        part = dot(member.astype(bf16), weights)
        rank_scr[s] = member * (part[:, :LANES] + before)
        before = before + part[:, LANES:]
    totals = before + 1.0
    high = jnp.floor(totals * (1.0 / 64.0))
    low = totals - 64.0 * high
    earlier = jnp.where(iota((BINS, BINS), 1) < iota((BINS, BINS), 0), 1.0, 0.0).astype(bf16)
    base = 64.0 * dot(earlier, high.astype(bf16)) + dot(earlier, low.astype(bf16))
    places = []
    for s in range(sources):
        data = load(s)
        bins = jnp.clip((data[1:2] * (BINS / 8.0)).astype(i32), 0, BINS - 1)
        here = data[12:13] > 0.5
        member = jnp.where(bins == iota((BINS, LANES), 0), base, 0.0)
        place = jnp.sum(member + rank_scr[s], axis=0, keepdims=True).astype(i32)
        places.append(jnp.where(here, place, -1))
    chunk, lane, here = invert(places, chunks)
    inv_chunk[...] = chunk
    inv_lane[...] = lane
    for d in range(chunks):
        own_ref[:, d * LANES : (d + 1) * LANES] = pick(
            load, sources, inv_chunk[d : d + 1, :], inv_lane[d : d + 1, :], inv_lane[d : d + 1, :] >= 0
        )
    share_ref[...] = jnp.zeros_like(share_ref)
    share_ref[0:8, :] = own_ref[4:12, :] * (own_ref[2:3, :] * (1.0 / 256.0))
    share_ref[8:10, :] = own_ref[0:2, :] * 4.0
    stat = jnp.zeros((1, LANES), f32)
    for axis in range(2):
        wide = jnp.concatenate(
            [share_ref[8 + axis : 9 + axis, c * LANES : (c + 1) * LANES] for c in range(chunks)], axis=0
        )
        for which, value in ((0, jnp.min(wide, axis=1, keepdims=True)), (1, jnp.max(wide, axis=1, keepdims=True))):
            lanes = iota((chunks, LANES), 1) - chunks * (2 * axis + which)
            stat = stat + jnp.sum(
                jnp.where(lanes == iota((chunks, LANES), 0), value, 0.0), axis=0, keepdims=True
            )
    stat = jnp.where(iota((1, LANES), 1) == 4 * chunks, count_ref[0].astype(f32), stat)
    share_ref[10:11, 0:LANES] = stat


def make_list(hops, tile_ref, shares, list_ref):
    chunks = list_ref.shape[0]
    my_tile = tile_ref[0]
    own = shares[hops][10:11, 0:LANES]
    lane, sub = iota((chunks, LANES), 1), iota((chunks, LANES), 0)
    x_low, x_high, y_low, y_high = [
        jnp.sum(jnp.where(lane == sub + chunks * q, own, 0.0), axis=1, keepdims=True) for q in range(4)
    ]
    own_count = own[:, 4 * chunks : 4 * chunks + 1]
    need = jnp.zeros((chunks, LANES), f32)
    for nb in range(2 * hops + 1):
        hop = nb - hops
        other = shares[nb][10:11, 0:LANES]
        at = [pltpu.roll(other, (nb * chunks - q * chunks) % LANES, 1) for q in range(4)]
        gap_x = jnp.maximum(jnp.maximum(at[0] - x_high, x_low - at[1]), 0.0)
        gap_y = jnp.maximum(jnp.maximum(at[2] - y_high, y_low - at[3]), 0.0)
        near = gap_x * gap_x + gap_y * gap_y < 16.001
        count = own_count if hop >= 0 else other[:, 4 * chunks : 4 * chunks + 1]
        listed = (count > abs(hop) + 0.5) & (my_tile + hop >= 0)
        inside = (lane >= nb * chunks) & (lane < (nb + 1) * chunks)
        need = need + jnp.where(near & listed & inside, 1.0, 0.0)
    total = dot(need.astype(bf16), running_sum_weights())
    slot = jnp.where(need > 0.5, total[:, :LANES] - 1.0, -1.0)
    numbers = jnp.broadcast_to(iota((8, LANES), 1).astype(f32), (8, LANES)).astype(bf16)
    for r in range(chunks):
        match = jnp.where(slot[r : r + 1] == iota((LANES, LANES), 0).astype(f32), 1.0, 0.0)
        found = dot_t(numbers, match.astype(bf16))[0:1]
        amount = total[r : r + 1, LANES:]
        row = jnp.where(iota((1, LANES), 1).astype(f32) < amount, found, float((2 * hops + 1) * chunks))
        row = jnp.where(iota((1, LANES), 1) == LANES - 1, amount, row)
        list_ref[r : r + 1, :] = row.astype(i32)


def load_operands(hops, shares, vectors, where_scr, vec_scr):
    chunks = shares[0].shape[1] // LANES
    for nb in range(2 * hops + 1):
        for c in range(chunks):
            lanes = slice(c * LANES, (c + 1) * LANES)
            where_scr[nb * chunks + c] = shares[nb][8:16, lanes]
            value = vectors[nb][0:8, lanes]
            high = value.astype(bf16)
            low = (value - high.astype(f32)).astype(bf16)
            vec_scr[nb * chunks + c] = jnp.concatenate([high, low], axis=0)
    last = (2 * hops + 1) * chunks
    where_scr[last] = jnp.zeros((8, LANES), f32)
    vec_scr[last] = jnp.zeros((16, LANES), bf16)


def product(hops, list_smem, where_scr, vec_scr, out_ref):
    chunks = out_ref.shape[1] // LANES

    def chunk_rows(r, _):
        column = where_scr[hops * chunks + r].T
        x_col = jnp.broadcast_to(column[:, 0:1], (LANES, LANES))
        y_col = jnp.broadcast_to(column[:, 1:2], (LANES, LANES))

        def batch(b, total):
            highs, lows, vecs = [], [], []
            for j in range(BATCH):
                c = list_smem[r, b * BATCH + j]
                dx = x_col - where_scr[c, 0:1, :]
                dy = y_col - where_scr[c, 1:2, :]
                square = jnp.maximum(dx * dx + dy * dy, 1e-30)
                distance = square * lax.rsqrt(square)
                inside = jnp.maximum(4.0 - distance, 0.0)
                inside = inside * inside
                corr = inside * inside * (distance + 1.0)
                high = corr.astype(bf16)
                highs.append(high)
                lows.append((corr - high.astype(f32)).astype(bf16))
                vecs.append(vec_scr[c])
            return total + dot_t(
                jnp.concatenate(highs + lows, axis=1), jnp.concatenate(vecs + vecs, axis=1)
            )

        steps = (list_smem[r, LANES - 1] + (BATCH - 1)) // BATCH
        total = lax.fori_loop(0, steps, batch, jnp.zeros((LANES, 16), f32))
        flat = total.T
        out_ref[:, pl.ds(pl.multiple_of(r * LANES, LANES), LANES)] = flat[0:8] + flat[8:16]
        return 0

    lax.fori_loop(0, chunks, chunk_rows, 0)


def first_kernel(hops, tile_ref, own_ref, *refs):
    shares = refs[: 2 * hops + 1]
    image_ref, share_ref, dots_ref, list_ref, list_smem, where_scr, vec_scr, sem = refs[2 * hops + 1 :]
    make_list(hops, tile_ref, shares, list_ref)
    copy = pltpu.make_async_copy(list_ref, list_smem, sem)
    copy.start()
    load_operands(hops, shares, shares, where_scr, vec_scr)
    copy.wait()
    product(hops, list_smem, where_scr, vec_scr, image_ref)
    field = own_ref[4:12, :]
    image = own_ref[3:4, :] * field + own_ref[2:3, :] * image_ref[...]
    image_ref[...] = image
    share_ref[...] = image * (own_ref[2:3, :] * (1.0 / 256.0))
    dots_ref[:, 0:128] = jnp.broadcast_to(jnp.sum(field * field, axis=1, keepdims=True), (8, LANES))
    dots_ref[:, 128:256] = jnp.broadcast_to(jnp.sum(field * image, axis=1, keepdims=True), (8, LANES))
    dots_ref[:, 256:384] = jnp.broadcast_to(jnp.sum(image * image, axis=1, keepdims=True), (8, LANES))


def second_kernel(hops, list_smem, own_ref, image_ref, *refs):
    n = 2 * hops + 1
    shares, vectors = refs[:n], refs[n : 2 * n]
    twice_ref, where_scr, vec_scr = refs[2 * n :]
    load_operands(hops, shares, vectors, where_scr, vec_scr)
    product(hops, list_smem, where_scr, vec_scr, twice_ref)
    twice_ref[...] = own_ref[3:4, :] * image_ref[...] + own_ref[2:3, :] * twice_ref[...]


def place_kernel(own_ref, data_ref, out_ref, inv_chunk, inv_lane):
    chunks = own_ref.shape[1] // LANES
    places = [own_ref[12:13, c * LANES : (c + 1) * LANES].astype(i32) - 1 for c in range(chunks)]
    chunk, lane, _ = invert(places, chunks)
    inv_chunk[...] = chunk
    inv_lane[...] = lane
    for d in range(chunks):
        out_ref[:, d * LANES : (d + 1) * LANES] = pick(
            lambda s: data_ref[:, s * LANES : (s + 1) * LANES],
            chunks,
            inv_chunk[d : d + 1, :],
            inv_lane[d : d + 1, :],
            inv_lane[d : d + 1, :] >= 0,
        )


def call(kernel, outs, ins, scratch=()):
    return pl.pallas_call(
        kernel,
        out_shape=[jax.ShapeDtypeStruct(shape, kind) for shape, kind in outs],
        in_specs=ins,
        out_specs=[VMEM] * len(outs),
        scratch_shapes=list(scratch),
        compiler_params=pltpu.CompilerParams(vmem_limit_bytes=LIMIT),
    )


def around(value, hops, tiles):
    got = {0: value}
    for hop in range(1, hops + 1):
        for sign in (1, -1):
            pairs = [(i, (i - sign * hop) % tiles) for i in range(tiles)]
            got[sign * hop] = lax.ppermute(value, "tiles", pairs)
    return [got[hop] for hop in range(-hops, hops + 1)]


def local(obs_position, obs_sd, obs_var, innovations, obs_target, pair_table, pair_count):
    tiles = lax.axis_size("tiles")
    my_tile = lax.axis_index("tiles").astype(i32)
    rows = obs_sd.shape[0]
    chunks = rows // LANES
    hops = pair_table.shape[1] - 1
    held = (2 * hops + 1) * chunks
    capacity = 3 * rows // (2 * tiles)
    width = -(-capacity // LANES) * LANES
    boxes = tiles * width // LANES

    (outbox,) = call(
        functools.partial(outbox_kernel, tiles, width),
        [((tiles, FIELDS, width), f32)],
        [VMEM] * 5,
        [pltpu.VMEM((FIELDS, rows), f32)] + [pltpu.VMEM((boxes, LANES), i32)] * 3,
    )(obs_position, obs_sd[None], obs_var[None], innovations, obs_target[None])
    inbox = lax.all_to_all(outbox, "tiles", split_axis=0, concat_axis=0, tiled=True)
    share, own = call(
        sort_kernel,
        [((FIELDS, rows), f32), ((FIELDS, rows), f32)],
        [VMEM, SMEM],
        [pltpu.VMEM((chunks, LANES), i32)] * 2 + [pltpu.VMEM((boxes, BINS, LANES), f32)],
    )(inbox, pair_count)
    shares = around(share, hops, tiles)
    operands = [pltpu.VMEM((held + 1, 8, LANES), f32), pltpu.VMEM((held + 1, 16, LANES), bf16)]
    image, image_share, dots, near = call(
        functools.partial(first_kernel, hops),
        [((8, rows), f32), ((8, rows), f32), ((8, 3 * LANES), f32), ((chunks, LANES), i32)],
        [SMEM] + [VMEM] * (2 * hops + 2),
        [pltpu.SMEM((chunks, LANES), i32)] + operands + [pltpu.SemaphoreType.DMA],
    )(my_tile[None], own, *shares)
    vectors = around(image_share, hops, tiles)
    (twice,) = call(
        functools.partial(second_kernel, hops),
        [((8, rows), f32)],
        [SMEM] + [VMEM] * (4 * hops + 4),
        operands,
    )(near, own, image, *shares, *vectors)

    sums = jnp.sum(lax.all_gather(dots, "tiles"), axis=0)
    norm, power, size = sums[:, 0:1], sums[:, 128:129], sums[:, 256:257]
    field = own[4:12]
    alpha = norm / power
    beta = (alpha * alpha * size - norm) / norm
    residual = field - alpha * image
    direction = residual + beta * field
    moved = (1.0 + beta) * image - alpha * twice
    parts = jnp.concatenate(
        [
            jnp.broadcast_to(jnp.sum(residual * residual, axis=1, keepdims=True), (8, 64)),
            jnp.broadcast_to(jnp.sum(direction * moved, axis=1, keepdims=True), (8, 64)),
        ],
        axis=1,
    )
    both = lax.all_to_all(
        jnp.broadcast_to(parts[None], (tiles, 8, LANES)), "tiles", split_axis=0, concat_axis=0, tiled=True
    )
    both = jnp.sum(both, axis=0)
    alpha_next = both[:, 0:1] / both[:, 64:65]
    data = jnp.concatenate(
        [alpha * field + alpha_next * direction, residual - alpha_next * moved], axis=0
    )
    (placed,) = call(
        place_kernel, [((16, rows), f32)], [VMEM, VMEM], [pltpu.VMEM((chunks, LANES), i32)] * 2
    )(own, data)
    return (placed[0:8], placed[8:16])


def solution(mesh):
    both = ("groups", "tiles")
    placed = (P(None, both), P(both), P(both), P(None, both), P(both), P(both, None, None), P(both))
    return jax.shard_map(
        local,
        mesh=mesh,
        in_specs=placed,
        out_specs=(P(None, both), P(None, both)),
        check_vma=False,
    )
```

time: 961 us -> 174 us (0.18); the launches traced: 950 us -> 174 us
  matrix products: 551 us -> 0 us
  starting transfers between devices: 225 us -> 42.4 us
  Pallas kernels: 0 us -> 49.1 us
  blocking collectives: 90.3 us -> 53 us
  local copies, waits for them, and re-layouts: 37.1 us -> 4.45 us
  other arithmetic: 18.6 us -> 0.89 us
    dot_general x192 -> x0, matrix products: 551 us -> none  [the longest x96 281 us: one_block(): lax.dot_general(dir_cols, block_corr, (((1,), (1,)), ((), ())), precision...]
    ppermute x15 -> x12, starting transfers between devices: 217 us -> 35 us  [around(): got[sign * hop] = lax.ppermute(value, 'tiles', pairs)]
    psum x3 -> x0, blocking collectives: 90.3 us -> none  [the longest x2 60.8 us: squares(): return lax.psum(jnp.sum(residual * residual, axis=1), 'tiles')]
    pallas_call x0 -> x5, Pallas kernels: none -> 49.1 us  [the longest x1 21.5 us: local(): call(functools.partial(first_kernel, hops), [((8, rows), f32), ((8, rows)...]
    all_to_all x0 -> x1, blocking collectives: none -> 31.9 us  [local(): lax.all_to_all(jnp.broadcast_to(parts[None], (tiles, 8, LANES)), 'tiles',...]
    all_gather x0 -> x1, blocking collectives: none -> 21.1 us  [local(): sums = jnp.sum(lax.all_gather(dots, 'tiles'), axis=0)]
    scatter x2 -> x0, local copies, waits for them, and re-layouts: 14.7 us -> none  [the longest x1 8.69 us: local(): arrived = jnp.zeros((fields.shape[0] - 1, tile_rows), jnp.float32).at[:,...]
    another operation x30 -> x0, local copies, waits for them, and re-layouts: 9.76 us -> none
  transfers between devices with their start and end apart: 16 -> 13, of which waited for: 7 -> 8; matrix products, arithmetic and copies ran while one was open for 1% -> 0% of each run, Pallas kernels for 0% -> 0%
where the time goes in v1:
time: 174 us
  blocking collectives  53 us (30%)
  Pallas kernels  49.1 us (28%)
  starting transfers between devices  42.4 us (24%)
  waiting for transfers between devices  23.2 us (13%)
  local copies, waits for them, and re-layouts  4.45 us (3%)
    ppermute x12, starting transfers between devices, around(): got[sign * hop] = lax.ppermute(value, 'tiles', pairs)  35 us
    all_to_all x1, blocking collectives, local(): lax.all_to_all(jnp.broadcast_to(parts[None], (tiles, 8, LANES)), 'tiles',...  31.9 us
    pallas_call x1, Pallas kernels, local(): call(functools.partial(first_kernel, hops), [((8, rows), f32), ((8, rows)...  21.5 us
    all_gather x1, blocking collectives, local(): sums = jnp.sum(lax.all_gather(dots, 'tiles'), axis=0)  21.1 us
    pallas_call x1, Pallas kernels, local(): call(functools.partial(second_kernel, hops), [((8, rows), f32)], [SMEM] +...  20.7 us
    ppermute x12, waiting for transfers between devices, around(): got[sign * hop] = lax.ppermute(value, 'tiles', pairs)  13.8 us
    all_to_all x1, waiting for transfers between devices, local(): lax.all_to_all(outbox, 'tiles', split_axis=0, concat_axis=0, tiled=True)  9.4 us
    all_to_all x1, starting transfers between devices, local(): lax.all_to_all(outbox, 'tiles', split_axis=0, concat_axis=0, tiled=True)  7.39 us
  transfers between devices with their start and end apart: 13, of which 8 were waited for; matrix products, arithmetic and copies ran while one was open for 0% of the time, Pallas kernels for 0%

profile of v1, /device:TPU:0, one launch (start us, length us, event | category | flops | bytes accessed | tf_op | source)
XLA Modules:
  0.0 174.4 jit_solution(7225717306222426400)
XLA Ops:
  0.6 0.0 copy-start
  0.6 0.8 copy-done
  1.5 0.7 copy-done.1
  2.2 0.7 copy-done.2
  2.9 0.7 copy-done.3
  3.6 0.7 copy-done.4
  4.3 2.4 %shard_map.77 = f32[16,16,256]{2,1,0:T(8,128)} custom-call(f32[2,2048]{1,0:T(2,128)S(1)} %copy-done.1, f32[1,2048]{1,0:T(1,128)S(1)} %bitcast.6, f32[1,2048]{1,0:T(1,128)S(1)} %bitcast.7, f32[8,2048]{1,0:T(8,128)S(1)} %copy-done, s32[1,2048]{1,0:T(1,128)S(1)} %bitcast.8), custom_call_target="tpu_custom_call" | custom-call | tf_op jit(solution)/shard_map/pallas_call | solution.py:324
  6.7 7.4 %all-to-all-start = ((f32[16,16,256]{2,1,0:T(8,128)}), f32[16,16,256]{2,1,0:T(8,128)S(1)}, u32[]{:S(2)}, u32[]{:S(2)}) async-start(f32[16,16,256]{2,1,0:T(8,128)} %shard_map.77), calls=%async_computation | async-start | bytes 524288 | tf_op jit(solution)/shard_map/all_to_all | solution.py:330
  14.8 9.4 %all-to-all-done.in_ref = f32[16,16,256]{2,1,0:T(8,128)S(1)} async-done(((f32[16,16,256]{2,1,0:T(8,128)}), f32[16,16,256]{2,1,0:T(8,128)S(1)}, u32[]{:S(2)}, u32[]{:S(2)}) %all-to-all-start) | async-done | bytes 262176 | tf_op jit(solution)/shard_map/all_to_all | solution.py:330
  24.2 3.5 %shard_map.78 = (f32[16,2048]{1,0:T(8,128)S(1)}, f32[16,2048]{1,0:T(8,128)S(1)}) custom-call(f32[16,16,256]{2,1,0:T(8,128)S(1)} %all-to-all-done.in_ref, s32[1]{0:T(128)S(6)} %copy.8.count_ref), custom_call_target="tpu_custom_call" | custom-call | tf_op jit(solution)/shard_map/pallas_call | solution.py:331
  27.7 1.0 collective-permute-start.5
  28.7 0.7 collective-permute-start.4
  29.4 0.8 collective-permute-start.3
  30.2 0.0 collective-permute-start.2
  30.2 1.5 collective-permute-start.1
  31.7 0.8 collective-permute-done.5.refs_6_
  32.5 1.1 collective-permute-start
  33.6 1.8 %collective-permute-done.4.refs_5_ = f32[16,2048]{1,0:T(8,128)S(1)} collective-permute-done((f32[16,2048]{1,0:T(8,128)S(1)}, f32[16,2048]{1,0:T(8,128)S(1)}, u32[]{:S(2)}, u32[]{:S(2)}) %collective-permute-start.4) | collective-permute-done | bytes 131104 | tf_op jit(solution)/shard_map/ppermute | solution.py:309
  35.3 2.8 %collective-permute-done.3.refs_4_ = f32[16,2048]{1,0:T(8,128)S(1)} collective-permute-done((f32[16,2048]{1,0:T(8,128)S(1)}, f32[16,2048]{1,0:T(8,128)S(1)}, u32[]{:S(2)}, u32[]{:S(2)}) %collective-permute-start.3) | collective-permute-done | bytes 131104 | tf_op jit(solution)/shard_map/ppermute | solution.py:309
  38.2 0.1 collective-permute-done.2.refs_2_
  38.2 1.1 collective-permute-done.1.refs_1_
  39.3 1.9 %collective-permute-done.refs_0_ = f32[16,2048]{1,0:T(8,128)S(1)} collective-permute-done((f32[16,2048]{1,0:T(8,128)S(1)}, f32[16,2048]{1,0:T(8,128)S(1)}, u32[]{:S(2)}, u32[]{:S(2)}) %collective-permute-start) | collective-permute-done | bytes 131104 | tf_op jit(solution)/shard_map/ppermute | solution.py:309
  41.2 21.5 %shard_map.79 = (f32[8,2048]{1,0:T(8,128)S(1)}, f32[8,2048]{1,0:T(8,128)S(1)}, f32[8,384]{1,0:T(8,128)S(1)}, s32[16,128]{1,0:T(8,128)S(1)}) custom-call(s32[1]{0:T(128)} %bitcast.3.tile_ref, f32[16,2048]{1,0:T(8,128)S(1)} %get-tuple-element.8.own_ref, f32[16,2048]{1,0:T(8,128)S(1)} %collective-permute-done.refs_0_, ...), custom_call_target="tpu_custom_call" | custom-call | tf_op jit(solution)/shard_map/pallas_call | solution.py:339
  62.7 27.4 %collective-permute-start.11 = (f32[8,2048]{1,0:T(8,128)S(1)}, f32[8,2048]{1,0:T(8,128)S(1)}, u32[]{:S(2)}, u32[]{:S(2)}) collective-permute-start(f32[8,2048]{1,0:T(8,128)S(1)} %get-tuple-element.13.refs_10_), channel_id=1, source_target_pairs={{0,13},{1,14},{2,15},{3,0},{4,1},{5,2},{6,3},{7,4},{8,5},{9,6},{10... | collective-permute-start | bytes 196616 | tf_op jit(solution)/shard_map/ppermute | solution.py:309
  90.0 0.0 collective-permute-start.10
  90.0 1.2 collective-permute-start.9
  91.3 0.0 collective-permute-start.8
  91.3 1.3 collective-permute-start.7
  92.6 21.1 %all-gather = f32[128,384]{1,0:T(8,128)S(1)} all-gather(f32[8,384]{1,0:T(8,128)S(1)} %get-tuple-element.10), channel_id=2, replica_groups=mesh['groups'=2,'tiles'=16] {'tiles'}, dimensions={0}, use_global_device_ids=true | all-gather | bytes 208896 | tf_op jit(solution)/shard_map/all_gather | solution.py:353
  113.7 0.1 subtract_divide_fusion
  113.8 0.0 collective-permute-done.11.refs_13_
  113.8 0.1 collective-permute-start.6
  113.9 0.1 add_reduce_fusion
  114.0 0.0 collective-permute-done.10.refs_12_
  114.0 0.0 collective-permute-done.9.refs_11_
  114.0 0.0 collective-permute-done.8.refs_9_
  114.0 0.0 collective-permute-done.7.refs_8_
  114.1 5.3 %collective-permute-done.6.refs_7_ = f32[8,2048]{1,0:T(8,128)S(1)} collective-permute-done((f32[8,2048]{1,0:T(8,128)S(1)}, f32[8,2048]{1,0:T(8,128)S(1)}, u32[]{:S(2)}, u32[]{:S(2)}) %collective-permute-start.6) | collective-permute-done | bytes 65568 | tf_op jit(solution)/shard_map/ppermute | solution.py:309
  119.3 20.7 %shard_map.80 = f32[8,2048]{1,0:T(8,128)S(1)} custom-call(s32[16,128]{1,0:T(8,128)S(1)} %get-tuple-element.12.list_smem, f32[16,2048]{1,0:T(8,128)S(1)} %get-tuple-element.8.own_ref, f32[8,2048]{1,0:T(8,128)S(1)} %get-tuple-element.11.image_ref, f32[16,2048]{1,0:T(8,128)S(1)} %collective-permute-done.refs_0_, f32[16,2048]{1,0:T(8,128)S(1)} %collective-permute-done.1.refs_1_, ...), custom_call_target="tpu_custom_call" | custom-call | tf_op jit(solution)/shard_map/pallas_call | solution.py:346
  140.0 0.2 multiply_reduce_fusion.1
  140.3 0.1 broadcast_in_dim.34
  140.3 0.1 broadcast_in_dim.35
  140.4 0.1 pad_maximum_fusion.1
  140.5 31.9 %all_to_all.10 = f32[16,8,128]{2,1,0:T(8,128)S(1)} all-to-all(f32[16,8,128]{2,1,0:T(8,128)S(1)} %broadcast_in_dim.36), channel_id=1, replica_groups=mesh['groups'=2,'tiles'=16] {'tiles'}, dimensions={0} | all-to-all | bytes 131072 | tf_op jit(solution)/shard_map/all_to_all | solution.py:368
  172.4 0.2 divide_reduce_fusion
  172.6 0.1 multiply_add_fusion
  172.8 1.0 shard_map.81
  173.7 0.7 fusion.1
  (8 shorter events, 0.1 us)
Async XLA Ops:
  0.6 0.8 copy-start
  1.5 0.7 copy-start.1
  2.2 0.7 copy-start.2
  2.9 0.7 copy-start.3
  3.6 0.7 copy-start.4
  6.7 17.4 %all-to-all-start = ((f32[16,16,256]{2,1,0:T(8,128)}), f32[16,16,256]{2,1,0:T(8,128)S(1)}, u32[]{:S(2)}, u32[]{:S(2)}) async-start(f32[16,16,256]{2,1,0:T(8,128)} %shard_map.77), calls=%async_computation | async-start | bytes 524288 | tf_op jit(solution)/shard_map/all_to_all | solution.py:330
  27.7 4.8 %collective-permute-start.5 = (f32[16,2048]{1,0:T(8,128)S(1)}, f32[16,2048]{1,0:T(8,128)S(1)}, u32[]{:S(2)}, u32[]{:S(2)}) collective-permute-start(f32[16,2048]{1,0:T(8,128)S(1)} %get-tuple-element.9.refs_3_), channel_id=1, source_target_pairs={{0,13},{1,14},{2,15},{3,0},{4,1},{5,2},{6,3},{7,4},{8,5},{9,6},{10... | collective-permute-start | bytes 393224 | tf_op jit(solution)/shard_map/ppermute | solution.py:309
  28.7 6.7 %collective-permute-start.4 = (f32[16,2048]{1,0:T(8,128)S(1)}, f32[16,2048]{1,0:T(8,128)S(1)}, u32[]{:S(2)}, u32[]{:S(2)}) collective-permute-start(f32[16,2048]{1,0:T(8,128)S(1)} %get-tuple-element.9.refs_3_), channel_id=1, source_target_pairs={{0,14},{1,15},{2,0},{3,1},{4,2},{5,3},{6,4},{7,5},{8,6},{9,7},{10,... | collective-permute-start | bytes 393224 | tf_op jit(solution)/shard_map/ppermute | solution.py:309
  29.4 8.8 %collective-permute-start.3 = (f32[16,2048]{1,0:T(8,128)S(1)}, f32[16,2048]{1,0:T(8,128)S(1)}, u32[]{:S(2)}, u32[]{:S(2)}) collective-permute-start(f32[16,2048]{1,0:T(8,128)S(1)} %get-tuple-element.9.refs_3_), channel_id=1, source_target_pairs={{0,15},{1,0},{2,1},{3,2},{4,3},{5,4},{6,5},{7,6},{8,7},{9,8},{10,9... | collective-permute-start | bytes 393224 | tf_op jit(solution)/shard_map/ppermute | solution.py:309
  30.2 8.0 %collective-permute-start.2 = (f32[16,2048]{1,0:T(8,128)S(1)}, f32[16,2048]{1,0:T(8,128)S(1)}, u32[]{:S(2)}, u32[]{:S(2)}) collective-permute-start(f32[16,2048]{1,0:T(8,128)S(1)} %get-tuple-element.9.refs_3_), channel_id=1, source_target_pairs={{0,1},{1,2},{2,3},{3,4},{4,5},{5,6},{6,7},{7,8},{8,9},{9,10},{10,1... | collective-permute-start | bytes 393224 | tf_op jit(solution)/shard_map/ppermute | solution.py:309
  30.2 9.1 %collective-permute-start.1 = (f32[16,2048]{1,0:T(8,128)S(1)}, f32[16,2048]{1,0:T(8,128)S(1)}, u32[]{:S(2)}, u32[]{:S(2)}) collective-permute-start(f32[16,2048]{1,0:T(8,128)S(1)} %get-tuple-element.9.refs_3_), channel_id=1, source_target_pairs={{0,2},{1,3},{2,4},{3,5},{4,6},{5,7},{6,8},{7,9},{8,10},{9,11},{10,... | collective-permute-start | bytes 393224 | tf_op jit(solution)/shard_map/ppermute | solution.py:309
  32.5 8.7 %collective-permute-start = (f32[16,2048]{1,0:T(8,128)S(1)}, f32[16,2048]{1,0:T(8,128)S(1)}, u32[]{:S(2)}, u32[]{:S(2)}) collective-permute-start(f32[16,2048]{1,0:T(8,128)S(1)} %get-tuple-element.9.refs_3_), channel_id=1, source_target_pairs={{0,3},{1,4},{2,5},{3,6},{4,7},{5,8},{6,9},{7,10},{8,11},{9,12},{10... | collective-permute-start | bytes 393224 | tf_op jit(solution)/shard_map/ppermute | solution.py:309
  62.7 51.1 %collective-permute-start.11 = (f32[8,2048]{1,0:T(8,128)S(1)}, f32[8,2048]{1,0:T(8,128)S(1)}, u32[]{:S(2)}, u32[]{:S(2)}) collective-permute-start(f32[8,2048]{1,0:T(8,128)S(1)} %get-tuple-element.13.refs_10_), channel_id=1, source_target_pairs={{0,13},{1,14},{2,15},{3,0},{4,1},{5,2},{6,3},{7,4},{8,5},{9,6},{10... | collective-permute-start | bytes 196616 | tf_op jit(solution)/shard_map/ppermute | solution.py:309
  90.0 24.0 %collective-permute-start.10 = (f32[8,2048]{1,0:T(8,128)S(1)}, f32[8,2048]{1,0:T(8,128)S(1)}, u32[]{:S(2)}, u32[]{:S(2)}) collective-permute-start(f32[8,2048]{1,0:T(8,128)S(1)} %get-tuple-element.13.refs_10_), channel_id=1, source_target_pairs={{0,14},{1,15},{2,0},{3,1},{4,2},{5,3},{6,4},{7,5},{8,6},{9,7},{10,... | collective-permute-start | bytes 196616 | tf_op jit(solution)/shard_map/ppermute | solution.py:309
  90.0 24.0 %collective-permute-start.9 = (f32[8,2048]{1,0:T(8,128)S(1)}, f32[8,2048]{1,0:T(8,128)S(1)}, u32[]{:S(2)}, u32[]{:S(2)}) collective-permute-start(f32[8,2048]{1,0:T(8,128)S(1)} %get-tuple-element.13.refs_10_), channel_id=1, source_target_pairs={{0,15},{1,0},{2,1},{3,2},{4,3},{5,4},{6,5},{7,6},{8,7},{9,8},{10,9... | collective-permute-start | bytes 196616 | tf_op jit(solution)/shard_map/ppermute | solution.py:309
  91.3 22.7 %collective-permute-start.8 = (f32[8,2048]{1,0:T(8,128)S(1)}, f32[8,2048]{1,0:T(8,128)S(1)}, u32[]{:S(2)}, u32[]{:S(2)}) collective-permute-start(f32[8,2048]{1,0:T(8,128)S(1)} %get-tuple-element.13.refs_10_), channel_id=1, source_target_pairs={{0,1},{1,2},{2,3},{3,4},{4,5},{5,6},{6,7},{7,8},{8,9},{9,10},{10,1... | collective-permute-start | bytes 196616 | tf_op jit(solution)/shard_map/ppermute | solution.py:309
  91.3 22.7 %collective-permute-start.7 = (f32[8,2048]{1,0:T(8,128)S(1)}, f32[8,2048]{1,0:T(8,128)S(1)}, u32[]{:S(2)}, u32[]{:S(2)}) collective-permute-start(f32[8,2048]{1,0:T(8,128)S(1)} %get-tuple-element.13.refs_10_), channel_id=1, source_target_pairs={{0,2},{1,3},{2,4},{3,5},{4,6},{5,7},{6,8},{7,9},{8,10},{9,11},{10,... | collective-permute-start | bytes 196616 | tf_op jit(solution)/shard_map/ppermute | solution.py:309
  113.8 5.5 %collective-permute-start.6 = (f32[8,2048]{1,0:T(8,128)S(1)}, f32[8,2048]{1,0:T(8,128)S(1)}, u32[]{:S(2)}, u32[]{:S(2)}) collective-permute-start(f32[8,2048]{1,0:T(8,128)S(1)} %get-tuple-element.13.refs_10_), channel_id=1, source_target_pairs={{0,3},{1,4},{2,5},{3,6},{4,7},{5,8},{6,9},{7,10},{8,11},{9,12},{10... | collective-permute-start | bytes 196616 | tf_op jit(solution)/shard_map/ppermute | solution.py:309

commit v2 on v1

--- a/solution.py
+++ b/solution.py
@@ -11,7 +11,7 @@
 LANES = 128
 FIELDS = 16
 BINS = 128
-BATCH = 4
+BATCH = 16
 TRANSPOSED = (((1,), (1,)), ((), ()))
 VMEM = pl.BlockSpec(memory_space=pltpu.VMEM)
 SMEM = pl.BlockSpec(memory_space=pltpu.SMEM)
@@ -66,18 +66,51 @@
 
 
 def outbox_kernel(
-    tiles, width, pos_ref, sd_ref, var_ref, innov_ref, target_ref, out_ref, fields, inv_chunk, inv_lane, inv_here
+    tiles,
+    width,
+    pos_ref,
+    sd_ref,
+    var_ref,
+    innov_ref,
+    target_ref,
+    out_ref,
+    fields,
+    pos_scr,
+    sd_scr,
+    var_scr,
+    innov_scr,
+    target_scr,
+    inv_chunk,
+    inv_lane,
+    inv_here,
+    sems,
 ):
     rows = pos_ref.shape[1]
     chunks = rows // LANES
+    copies = [
+        pltpu.make_async_copy(source, target, sems.at[k])
+        for k, (source, target) in enumerate(
+            (
+                (target_ref, target_scr),
+                (pos_ref, pos_scr),
+                (sd_ref, sd_scr),
+                (var_ref, var_scr),
+                (innov_ref, innov_scr),
+            )
+        )
+    ]
+    for copy in copies:
+        copy.start()
     fields[...] = jnp.zeros_like(fields)
-    fields[0:2, :] = pos_ref[...]
-    fields[2:3, :] = sd_ref[...]
-    fields[3:4, :] = var_ref[...]
-    target = target_ref[...]
+    for copy in copies:
+        copy.wait()
+    fields[0:2, :] = pos_scr[...]
+    fields[2:3, :] = sd_scr[...]
+    fields[3:4, :] = var_scr[...]
+    target = target_scr[...]
     owner = target // rows
     fields[12:13, :] = (target - owner * rows + 1).astype(f32)
-    fields[4:12, :] = innov_ref[...]
+    fields[4:12, :] = innov_scr[...]
     mine = [
         jnp.where(owner[:, c * LANES : (c + 1) * LANES] == iota((tiles, LANES), 0), 1.0, 0.0)
         for c in range(chunks)
@@ -219,10 +252,10 @@
         x_col = jnp.broadcast_to(column[:, 0:1], (LANES, LANES))
         y_col = jnp.broadcast_to(column[:, 1:2], (LANES, LANES))
 
-        def batch(b, total):
+        def batch(start, size, total):
             highs, lows, vecs = [], [], []
-            for j in range(BATCH):
-                c = list_smem[r, b * BATCH + j]
+            for j in range(size):
+                c = list_smem[r, start + j]
                 dx = x_col - where_scr[c, 0:1, :]
                 dy = y_col - where_scr[c, 1:2, :]
                 square = jnp.maximum(dx * dx + dy * dy, 1e-30)
@@ -234,14 +267,21 @@
                 highs.append(high)
                 lows.append((corr - high.astype(f32)).astype(bf16))
                 vecs.append(vec_scr[c])
-            return total + dot_t(
-                jnp.concatenate(highs + lows, axis=1), jnp.concatenate(vecs + vecs, axis=1)
+            vec = jnp.concatenate(vecs, axis=1)
+            total = total + dot_t(vec, jnp.concatenate(highs, axis=1))
+            return total + dot_t(vec, jnp.concatenate(lows, axis=1))
+
+        amount = list_smem[r, LANES - 1]
+        full = amount // BATCH
+        total = lax.fori_loop(
+            0, full, lambda b, t: batch(b * BATCH, BATCH, t), jnp.zeros((16, LANES), f32)
+        )
+        left = (amount - full * BATCH + 3) // 4
+        for size in range(4, BATCH + 1, 4):
+            total = lax.cond(
+                left == size // 4, lambda t, size=size: batch(full * BATCH, size, t), lambda t: t, total
             )
-
-        steps = (list_smem[r, LANES - 1] + (BATCH - 1)) // BATCH
-        total = lax.fori_loop(0, steps, batch, jnp.zeros((LANES, 16), f32))
-        flat = total.T
-        out_ref[:, pl.ds(pl.multiple_of(r * LANES, LANES), LANES)] = flat[0:8] + flat[8:16]
+        out_ref[:, pl.ds(pl.multiple_of(r * LANES, LANES), LANES)] = total[0:8] + total[8:16]
         return 0
 
     lax.fori_loop(0, chunks, chunk_rows, 0)
@@ -260,9 +300,17 @@
     image = own_ref[3:4, :] * field + own_ref[2:3, :] * image_ref[...]
     image_ref[...] = image
     share_ref[...] = image * (own_ref[2:3, :] * (1.0 / 256.0))
-    dots_ref[:, 0:128] = jnp.broadcast_to(jnp.sum(field * field, axis=1, keepdims=True), (8, LANES))
-    dots_ref[:, 128:256] = jnp.broadcast_to(jnp.sum(field * image, axis=1, keepdims=True), (8, LANES))
-    dots_ref[:, 256:384] = jnp.broadcast_to(jnp.sum(image * image, axis=1, keepdims=True), (8, LANES))
+    lane = iota((8, LANES), 1)
+    dots = jnp.where(
+        lane == 0,
+        jnp.sum(field * field, axis=1, keepdims=True),
+        jnp.where(
+            lane == 1,
+            jnp.sum(field * image, axis=1, keepdims=True),
+            jnp.sum(image * image, axis=1, keepdims=True),
+        ),
+    )
+    dots_ref[...] = jnp.broadcast_to(dots[None], dots_ref.shape)
 
 
 def second_kernel(hops, list_smem, own_ref, image_ref, *refs):
@@ -274,30 +322,40 @@
     twice_ref[...] = own_ref[3:4, :] * image_ref[...] + own_ref[2:3, :] * twice_ref[...]
 
 
-def place_kernel(own_ref, data_ref, out_ref, inv_chunk, inv_lane):
+def place_kernel(
+    own_ref, both_ref, alpha_ref, direction_ref, residual_ref, moved_ref, field_out, residual_out, inv_chunk, inv_lane, data_scr
+):
     chunks = own_ref.shape[1] // LANES
+    sums = both_ref[0]
+    for t in range(1, both_ref.shape[0]):
+        sums = sums + both_ref[t]
+    alpha_next = sums[:, 0:1] / sums[:, 1:2]
+    data_scr[0:8, :] = alpha_ref[:, 0:1] * own_ref[4:12, :] + alpha_next * direction_ref[...]
+    data_scr[8:16, :] = residual_ref[...] - alpha_next * moved_ref[...]
     places = [own_ref[12:13, c * LANES : (c + 1) * LANES].astype(i32) - 1 for c in range(chunks)]
     chunk, lane, _ = invert(places, chunks)
     inv_chunk[...] = chunk
     inv_lane[...] = lane
     for d in range(chunks):
-        out_ref[:, d * LANES : (d + 1) * LANES] = pick(
-            lambda s: data_ref[:, s * LANES : (s + 1) * LANES],
+        value = pick(
+            lambda s: data_scr[:, s * LANES : (s + 1) * LANES],
             chunks,
             inv_chunk[d : d + 1, :],
             inv_lane[d : d + 1, :],
             inv_lane[d : d + 1, :] >= 0,
         )
-
-
-def call(kernel, outs, ins, scratch=()):
+        field_out[:, d * LANES : (d + 1) * LANES] = value[0:8]
+        residual_out[:, d * LANES : (d + 1) * LANES] = value[8:16]
+
+
+def call(kernel, outs, ins, scratch=(), limit=LIMIT):
     return pl.pallas_call(
         kernel,
         out_shape=[jax.ShapeDtypeStruct(shape, kind) for shape, kind in outs],
         in_specs=ins,
         out_specs=[VMEM] * len(outs),
         scratch_shapes=list(scratch),
-        compiler_params=pltpu.CompilerParams(vmem_limit_bytes=LIMIT),
+        compiler_params=pltpu.CompilerParams(vmem_limit_bytes=limit),
     )
 
 
@@ -324,8 +382,18 @@
     (outbox,) = call(
         functools.partial(outbox_kernel, tiles, width),
         [((tiles, FIELDS, width), f32)],
-        [VMEM] * 5,
-        [pltpu.VMEM((FIELDS, rows), f32)] + [pltpu.VMEM((boxes, LANES), i32)] * 3,
+        [pl.BlockSpec(memory_space=pltpu.HBM)] * 5,
+        [
+            pltpu.VMEM((FIELDS, rows), f32),
+            pltpu.VMEM((2, rows), f32),
+            pltpu.VMEM((1, rows), f32),
+            pltpu.VMEM((1, rows), f32),
+            pltpu.VMEM((8, rows), f32),
+            pltpu.VMEM((1, rows), i32),
+        ]
+        + [pltpu.VMEM((boxes, LANES), i32)] * 3
+        + [pltpu.SemaphoreType.DMA((5,))],
+        64 * 2**20 - 2**16,
     )(obs_position, obs_sd[None], obs_var[None], innovations, obs_target[None])
     inbox = lax.all_to_all(outbox, "tiles", split_axis=0, concat_axis=0, tiled=True)
     share, own = call(
@@ -338,7 +406,7 @@
     operands = [pltpu.VMEM((held + 1, 8, LANES), f32), pltpu.VMEM((held + 1, 16, LANES), bf16)]
     image, image_share, dots, near = call(
         functools.partial(first_kernel, hops),
-        [((8, rows), f32), ((8, rows), f32), ((8, 3 * LANES), f32), ((chunks, LANES), i32)],
+        [((8, rows), f32), ((8, rows), f32), ((tiles, 8, LANES), f32), ((chunks, LANES), i32)],
         [SMEM] + [VMEM] * (2 * hops + 2),
         [pltpu.SMEM((chunks, LANES), i32)] + operands + [pltpu.SemaphoreType.DMA],
     )(my_tile[None], own, *shares)
@@ -350,33 +418,32 @@
         operands,
     )(near, own, image, *shares, *vectors)
 
-    sums = jnp.sum(lax.all_gather(dots, "tiles"), axis=0)
-    norm, power, size = sums[:, 0:1], sums[:, 128:129], sums[:, 256:257]
+    sums = jnp.sum(
+        lax.all_to_all(dots, "tiles", split_axis=0, concat_axis=0, tiled=True), axis=0
+    )
+    norm, power, size = sums[:, 0:1], sums[:, 1:2], sums[:, 2:3]
     field = own[4:12]
     alpha = norm / power
     beta = (alpha * alpha * size - norm) / norm
     residual = field - alpha * image
     direction = residual + beta * field
     moved = (1.0 + beta) * image - alpha * twice
-    parts = jnp.concatenate(
-        [
-            jnp.broadcast_to(jnp.sum(residual * residual, axis=1, keepdims=True), (8, 64)),
-            jnp.broadcast_to(jnp.sum(direction * moved, axis=1, keepdims=True), (8, 64)),
-        ],
-        axis=1,
+    parts = jnp.where(
+        jnp.arange(LANES)[None] == 0,
+        jnp.sum(residual * residual, axis=1, keepdims=True),
+        jnp.sum(direction * moved, axis=1, keepdims=True),
     )
     both = lax.all_to_all(
         jnp.broadcast_to(parts[None], (tiles, 8, LANES)), "tiles", split_axis=0, concat_axis=0, tiled=True
     )
-    both = jnp.sum(both, axis=0)
-    alpha_next = both[:, 0:1] / both[:, 64:65]
-    data = jnp.concatenate(
-        [alpha * field + alpha_next * direction, residual - alpha_next * moved], axis=0
-    )
-    (placed,) = call(
-        place_kernel, [((16, rows), f32)], [VMEM, VMEM], [pltpu.VMEM((chunks, LANES), i32)] * 2
-    )(own, data)
-    return (placed[0:8], placed[8:16])
+    return tuple(
+        call(
+            place_kernel,
+            [((8, rows), f32)] * 2,
+            [VMEM] * 6,
+            [pltpu.VMEM((chunks, LANES), i32)] * 2 + [pltpu.VMEM((16, rows), f32)],
+        )(own, both, jnp.broadcast_to(alpha, (8, LANES)), direction, residual, moved)
+    )
 
 
 def solution(mesh):

time: 174 us -> 129 us (0.74); the launches traced: 174 us -> 127 us
  blocking collectives: 53 us -> 20.6 us
  starting transfers between devices: 42.4 us -> 35.6 us
  local copies, waits for them, and re-layouts: 4.45 us -> 0.08 us
  Pallas kernels: 49.1 us -> 46.6 us
    all_gather x1 -> x0, blocking collectives: 21.1 us -> none  [local(): sums = jnp.sum(lax.all_gather(dots, 'tiles'), axis=0)]
    ppermute x12, starting transfers between devices: 35 us -> 16.2 us  [around(): got[sign * hop] = lax.ppermute(value, 'tiles', pairs)]
    all_to_all x0 -> x1, starting transfers between devices: none -> 11.9 us  [local(): lax.all_to_all(dots, 'tiles', split_axis=0, concat_axis=0, tiled=True)]
    all_to_all x1, blocking collectives: 31.9 us -> 20.6 us  [local(): lax.all_to_all(jnp.broadcast_to(parts[None], (tiles, 8, LANES)), 'tiles',...]
    unnamed x10 -> x0, local copies, waits for them, and re-layouts: 3.64 us -> none
    pallas_call x1, Pallas kernels: 20.7 us -> 18.4 us  [local(): call(functools.partial(second_kernel, hops), [((8, rows), f32)], [SMEM] +...]
    pallas_call x1, Pallas kernels: 21.5 us -> 19.7 us  [local(): call(functools.partial(first_kernel, hops), [((8, rows), f32), ((8, rows)...]
  transfers between devices with their start and end apart: 13 -> 14, of which waited for: 8 -> 6; matrix products, arithmetic and copies ran while one was open for 0% -> 0% of each run, Pallas kernels for 0% -> 14%
where the time goes in v2:
time: 129 us; the launch traced here: 127 us
  Pallas kernels  46.6 us (36%)
  starting transfers between devices  35.6 us (28%)
  waiting for transfers between devices  22.3 us (17%)
  blocking collectives  20.6 us (16%)
  between operations  1.35 us (1%)
    all_to_all x1, blocking collectives, local(): lax.all_to_all(jnp.broadcast_to(parts[None], (tiles, 8, LANES)), 'tiles',...  20.6 us
    pallas_call x1, Pallas kernels, local(): call(functools.partial(first_kernel, hops), [((8, rows), f32), ((8, rows)...  19.7 us
    pallas_call x1, Pallas kernels, local(): call(functools.partial(second_kernel, hops), [((8, rows), f32)], [SMEM] +...  18.4 us
    ppermute x12, starting transfers between devices, around(): got[sign * hop] = lax.ppermute(value, 'tiles', pairs)  16.2 us
    ppermute x12, waiting for transfers between devices, around(): got[sign * hop] = lax.ppermute(value, 'tiles', pairs)  12.9 us
    all_to_all x1, starting transfers between devices, local(): lax.all_to_all(dots, 'tiles', split_axis=0, concat_axis=0, tiled=True)  11.9 us
    all_to_all x1, waiting for transfers between devices, local(): lax.all_to_all(outbox, 'tiles', split_axis=0, concat_axis=0, tiled=True)  9.4 us
    all_to_all x1, starting transfers between devices, local(): lax.all_to_all(outbox, 'tiles', split_axis=0, concat_axis=0, tiled=True)  7.4 us
  transfers between devices with their start and end apart: 14, of which 6 were waited for; matrix products, arithmetic and copies ran while one was open for 0% of the time, Pallas kernels for 14%

profile of v2, /device:TPU:0, one launch (start us, length us, event | category | flops | bytes accessed | tf_op | source)
XLA Modules:
  0.0 127.4 jit_solution(13305269103314281606)
XLA Ops:
  0.6 3.4 %shard_map.77 = f32[16,16,256]{2,1,0:T(8,128)} custom-call(f32[2,2048]{1,0:T(2,128)} %pos_ref.1, f32[1,2048]{1,0:T(1,128)} %bitcast.4, f32[1,2048]{1,0:T(1,128)} %bitcast.5, f32[8,2048]{1,0:T(8,128)} %innov_ref.1, s32[1,2048]{1,0:T(1,128)} %bitcast.6), custom_call_target="tpu_custom_call" | custom-call | tf_op jit(solution)/shard_map/pallas_call | solution.py:382
  4.0 7.4 %all-to-all-start = ((f32[16,16,256]{2,1,0:T(8,128)}), f32[16,16,256]{2,1,0:T(8,128)S(1)}, u32[]{:S(2)}, u32[]{:S(2)}) async-start(f32[16,16,256]{2,1,0:T(8,128)} %shard_map.77), calls=%async_computation | async-start | bytes 524288 | tf_op jit(solution)/shard_map/all_to_all | solution.py:398
  12.1 9.4 %all-to-all-done.in_ref = f32[16,16,256]{2,1,0:T(8,128)S(1)} async-done(((f32[16,16,256]{2,1,0:T(8,128)}), f32[16,16,256]{2,1,0:T(8,128)S(1)}, u32[]{:S(2)}, u32[]{:S(2)}) %all-to-all-start) | async-done | bytes 262176 | tf_op jit(solution)/shard_map/all_to_all | solution.py:398
  21.5 3.5 %shard_map.78 = (f32[16,2048]{1,0:T(8,128)S(1)}, f32[16,2048]{1,0:T(8,128)S(1)}) custom-call(f32[16,16,256]{2,1,0:T(8,128)S(1)} %all-to-all-done.in_ref, s32[1]{0:T(128)S(6)} %copy.8.count_ref), custom_call_target="tpu_custom_call" | custom-call | tf_op jit(solution)/shard_map/pallas_call | solution.py:399
  25.0 0.2 collective-permute-start
  25.2 1.6 %collective-permute-start.1 = (f32[16,2048]{1,0:T(8,128)S(1)}, f32[16,2048]{1,0:T(8,128)S(1)}, u32[]{:S(2)}, u32[]{:S(2)}) collective-permute-start(f32[16,2048]{1,0:T(8,128)S(1)} %get-tuple-element.9.refs_3_), channel_id=1, source_target_pairs={{0,2},{1,3},{2,4},{3,5},{4,6},{5,7},{6,8},{7,9},{8,10},{9,11},{10,... | collective-permute-start | bytes 393224 | tf_op jit(solution)/shard_map/ppermute | solution.py:367
  26.8 0.0 collective-permute-start.2
  26.8 4.4 %collective-permute-start.3 = (f32[16,2048]{1,0:T(8,128)S(1)}, f32[16,2048]{1,0:T(8,128)S(1)}, u32[]{:S(2)}, u32[]{:S(2)}) collective-permute-start(f32[16,2048]{1,0:T(8,128)S(1)} %get-tuple-element.9.refs_3_), channel_id=1, source_target_pairs={{0,15},{1,0},{2,1},{3,2},{4,3},{5,4},{6,5},{7,6},{8,7},{9,8},{10,9... | collective-permute-start | bytes 393224 | tf_op jit(solution)/shard_map/ppermute | solution.py:367
  31.3 0.4 collective-permute-start.4
  31.7 0.0 collective-permute-done.refs_0_
  31.7 0.5 collective-permute-start.5
  32.2 5.1 %collective-permute-done.1.refs_1_ = f32[16,2048]{1,0:T(8,128)S(1)} collective-permute-done((f32[16,2048]{1,0:T(8,128)S(1)}, f32[16,2048]{1,0:T(8,128)S(1)}, u32[]{:S(2)}, u32[]{:S(2)}) %collective-permute-start.1) | collective-permute-done | bytes 131104 | tf_op jit(solution)/shard_map/ppermute | solution.py:367
  37.3 0.0 collective-permute-done.2.refs_2_
  37.3 0.0 collective-permute-done.3.refs_4_
  37.3 4.2 %collective-permute-done.4.refs_5_ = f32[16,2048]{1,0:T(8,128)S(1)} collective-permute-done((f32[16,2048]{1,0:T(8,128)S(1)}, f32[16,2048]{1,0:T(8,128)S(1)}, u32[]{:S(2)}, u32[]{:S(2)}) %collective-permute-start.4) | collective-permute-done | bytes 131104 | tf_op jit(solution)/shard_map/ppermute | solution.py:367
  41.5 0.0 collective-permute-done.5.refs_6_
  41.5 19.7 %shard_map.79 = (f32[8,2048]{1,0:T(8,128)S(1)}, f32[8,2048]{1,0:T(8,128)S(1)}, f32[16,8,128]{2,1,0:T(8,128)}, s32[16,128]{1,0:T(8,128)S(1)}) custom-call(s32[1]{0:T(128)} %bitcast.3.tile_ref, f32[16,2048]{1,0:T(8,128)S(1)} %get-tuple-element.8.own_ref, f32[16,2048]{1,0:T(8,128)S(1)} %collective-permute-done.refs_0_, ...), custom_call_target="tpu_custom_call" | custom-call | tf_op jit(solution)/shard_map/pallas_call | solution.py:407
  61.3 1.5 %collective-permute-start.6 = (f32[8,2048]{1,0:T(8,128)S(1)}, f32[8,2048]{1,0:T(8,128)S(1)}, u32[]{:S(2)}, u32[]{:S(2)}) collective-permute-start(f32[8,2048]{1,0:T(8,128)S(1)} %get-tuple-element.13.refs_10_), channel_id=1, source_target_pairs={{0,3},{1,4},{2,5},{3,6},{4,7},{5,8},{6,9},{7,10},{8,11},{9,12},{10... | collective-permute-start | bytes 196616 | tf_op jit(solution)/shard_map/ppermute | solution.py:367
  62.7 11.9 %all-to-all-start.1 = ((f32[16,8,128]{2,1,0:T(8,128)}), f32[16,8,128]{2,1,0:T(8,128)S(1)}, u32[]{:S(2)}, u32[]{:S(2)}) async-start(f32[16,8,128]{2,1,0:T(8,128)} %get-tuple-element.10), calls=%async_computation.1 | async-start | bytes 131072 | tf_op jit(solution)/shard_map/all_to_all | solution.py:422
  74.6 1.9 %collective-permute-start.7 = (f32[8,2048]{1,0:T(8,128)S(1)}, f32[8,2048]{1,0:T(8,128)S(1)}, u32[]{:S(2)}, u32[]{:S(2)}) collective-permute-start(f32[8,2048]{1,0:T(8,128)S(1)} %get-tuple-element.13.refs_10_), channel_id=1, source_target_pairs={{0,2},{1,3},{2,4},{3,5},{4,6},{5,7},{6,8},{7,9},{8,10},{9,11},{10,... | collective-permute-start | bytes 196616 | tf_op jit(solution)/shard_map/ppermute | solution.py:367
  76.6 0.0 collective-permute-start.8
  76.6 4.4 %collective-permute-start.9 = (f32[8,2048]{1,0:T(8,128)S(1)}, f32[8,2048]{1,0:T(8,128)S(1)}, u32[]{:S(2)}, u32[]{:S(2)}) collective-permute-start(f32[8,2048]{1,0:T(8,128)S(1)} %get-tuple-element.13.refs_10_), channel_id=1, source_target_pairs={{0,15},{1,0},{2,1},{3,2},{4,3},{5,4},{6,5},{7,6},{8,7},{9,8},{10,9... | collective-permute-start | bytes 196616 | tf_op jit(solution)/shard_map/ppermute | solution.py:367
  81.0 0.2 collective-permute-start.10
  81.2 0.0 collective-permute-done.6.refs_7_
  81.2 1.1 collective-permute-start.11
  82.2 1.2 collective-permute-done.7.refs_8_
  83.5 0.2 collective-permute-done.8.refs_9_
  83.7 0.0 collective-permute-done.9.refs_11_
  83.7 2.1 %collective-permute-done.10.refs_12_ = f32[8,2048]{1,0:T(8,128)S(1)} collective-permute-done((f32[8,2048]{1,0:T(8,128)S(1)}, f32[8,2048]{1,0:T(8,128)S(1)}, u32[]{:S(2)}, u32[]{:S(2)}) %collective-permute-start.10) | collective-permute-done | bytes 65568 | tf_op jit(solution)/shard_map/ppermute | solution.py:367
  85.8 0.0 collective-permute-done.11.refs_13_
  85.8 18.4 %shard_map.80 = f32[8,2048]{1,0:T(8,128)S(1)} custom-call(s32[16,128]{1,0:T(8,128)S(1)} %get-tuple-element.12.list_smem, f32[16,2048]{1,0:T(8,128)S(1)} %get-tuple-element.8.own_ref, f32[8,2048]{1,0:T(8,128)S(1)} %get-tuple-element.11.image_ref, f32[16,2048]{1,0:T(8,128)S(1)} %collective-permute-done.refs_0_, f32[16,2048]{1,0:T(8,128)S(1)} %collective-permute-done.1.refs_1_, ...), custom_call_target="tpu_custom_call" | custom-call | tf_op jit(solution)/shard_map/pallas_call | solution.py:414
  104.2 0.0 all-to-all-done.1
  104.3 0.2 subtract_divide_fusion
  104.5 0.1 add_reduce_fusion
  104.6 0.2 multiply_reduce_fusion.1
  104.8 0.2 multiply_reduce_fusion
  105.0 0.1 broadcast_select_fusion
  105.1 20.6 %all_to_all.15.both_ref = f32[16,8,128]{2,1,0:T(8,128)S(1)} all-to-all(f32[16,8,128]{2,1,0:T(8,128)S(1)} %broadcast_in_dim.57), channel_id=1, replica_groups=mesh['groups'=2,'tiles'=16] {'tiles'}, dimensions={0} | all-to-all | bytes 131072 | tf_op jit(solution)/shard_map/all_to_all | solution.py:436
  125.7 0.1 broadcast_in_dim.58.alpha_ref
  125.8 1.6 %shard_map.81 = (f32[8,2048]{1,0:T(8,128)}, f32[8,2048]{1,0:T(8,128)}) custom-call(f32[16,2048]{1,0:T(8,128)S(1)} %get-tuple-element.8.own_ref, f32[16,8,128]{2,1,0:T(8,128)S(1)} %all_to_all.15.both_ref, f32[8,128]{1,0:T(8,128)S(1)} %broadcast_in_dim.58.alpha_ref, f32[8,2048]{1,0:T(8,128)S(1)} %get-tuple-element.20.direction_ref, ...), custom_call_target="tpu_custom_call" | custom-call | tf_op jit(solution)/shard_map/pallas_call | solution.py:440
  (3 shorter events, 0.0 us)
Async XLA Ops:
  4.0 17.5 %all-to-all-start = ((f32[16,16,256]{2,1,0:T(8,128)}), f32[16,16,256]{2,1,0:T(8,128)S(1)}, u32[]{:S(2)}, u32[]{:S(2)}) async-start(f32[16,16,256]{2,1,0:T(8,128)} %shard_map.77), calls=%async_computation | async-start | bytes 524288 | tf_op jit(solution)/shard_map/all_to_all | solution.py:398
  25.0 6.7 %collective-permute-start = (f32[16,2048]{1,0:T(8,128)S(1)}, f32[16,2048]{1,0:T(8,128)S(1)}, u32[]{:S(2)}, u32[]{:S(2)}) collective-permute-start(f32[16,2048]{1,0:T(8,128)S(1)} %get-tuple-element.9.refs_3_), channel_id=1, source_target_pairs={{0,3},{1,4},{2,5},{3,6},{4,7},{5,8},{6,9},{7,10},{8,11},{9,12},{10... | collective-permute-start | bytes 393224 | tf_op jit(solution)/shard_map/ppermute | solution.py:367
  25.2 12.2 %collective-permute-start.1 = (f32[16,2048]{1,0:T(8,128)S(1)}, f32[16,2048]{1,0:T(8,128)S(1)}, u32[]{:S(2)}, u32[]{:S(2)}) collective-permute-start(f32[16,2048]{1,0:T(8,128)S(1)} %get-tuple-element.9.refs_3_), channel_id=1, source_target_pairs={{0,2},{1,3},{2,4},{3,5},{4,6},{5,7},{6,8},{7,9},{8,10},{9,11},{10,... | collective-permute-start | bytes 393224 | tf_op jit(solution)/shard_map/ppermute | solution.py:367
  26.8 10.5 %collective-permute-start.2 = (f32[16,2048]{1,0:T(8,128)S(1)}, f32[16,2048]{1,0:T(8,128)S(1)}, u32[]{:S(2)}, u32[]{:S(2)}) collective-permute-start(f32[16,2048]{1,0:T(8,128)S(1)} %get-tuple-element.9.refs_3_), channel_id=1, source_target_pairs={{0,1},{1,2},{2,3},{3,4},{4,5},{5,6},{6,7},{7,8},{8,9},{9,10},{10,1... | collective-permute-start | bytes 393224 | tf_op jit(solution)/shard_map/ppermute | solution.py:367
  26.8 10.5 %collective-permute-start.3 = (f32[16,2048]{1,0:T(8,128)S(1)}, f32[16,2048]{1,0:T(8,128)S(1)}, u32[]{:S(2)}, u32[]{:S(2)}) collective-permute-start(f32[16,2048]{1,0:T(8,128)S(1)} %get-tuple-element.9.refs_3_), channel_id=1, source_target_pairs={{0,15},{1,0},{2,1},{3,2},{4,3},{5,4},{6,5},{7,6},{8,7},{9,8},{10,9... | collective-permute-start | bytes 393224 | tf_op jit(solution)/shard_map/ppermute | solution.py:367
  31.3 10.3 %collective-permute-start.4 = (f32[16,2048]{1,0:T(8,128)S(1)}, f32[16,2048]{1,0:T(8,128)S(1)}, u32[]{:S(2)}, u32[]{:S(2)}) collective-permute-start(f32[16,2048]{1,0:T(8,128)S(1)} %get-tuple-element.9.refs_3_), channel_id=1, source_target_pairs={{0,14},{1,15},{2,0},{3,1},{4,2},{5,3},{6,4},{7,5},{8,6},{9,7},{10,... | collective-permute-start | bytes 393224 | tf_op jit(solution)/shard_map/ppermute | solution.py:367
  31.7 9.9 %collective-permute-start.5 = (f32[16,2048]{1,0:T(8,128)S(1)}, f32[16,2048]{1,0:T(8,128)S(1)}, u32[]{:S(2)}, u32[]{:S(2)}) collective-permute-start(f32[16,2048]{1,0:T(8,128)S(1)} %get-tuple-element.9.refs_3_), channel_id=1, source_target_pairs={{0,13},{1,14},{2,15},{3,0},{4,1},{5,2},{6,3},{7,4},{8,5},{9,6},{10... | collective-permute-start | bytes 393224 | tf_op jit(solution)/shard_map/ppermute | solution.py:367
  61.3 19.9 %collective-permute-start.6 = (f32[8,2048]{1,0:T(8,128)S(1)}, f32[8,2048]{1,0:T(8,128)S(1)}, u32[]{:S(2)}, u32[]{:S(2)}) collective-permute-start(f32[8,2048]{1,0:T(8,128)S(1)} %get-tuple-element.13.refs_10_), channel_id=1, source_target_pairs={{0,3},{1,4},{2,5},{3,6},{4,7},{5,8},{6,9},{7,10},{8,11},{9,12},{10... | collective-permute-start | bytes 196616 | tf_op jit(solution)/shard_map/ppermute | solution.py:367
  62.7 41.5 %all-to-all-start.1 = ((f32[16,8,128]{2,1,0:T(8,128)}), f32[16,8,128]{2,1,0:T(8,128)S(1)}, u32[]{:S(2)}, u32[]{:S(2)}) async-start(f32[16,8,128]{2,1,0:T(8,128)} %get-tuple-element.10), calls=%async_computation.1 | async-start | bytes 131072 | tf_op jit(solution)/shard_map/all_to_all | solution.py:422
  74.6 8.8 %collective-permute-start.7 = (f32[8,2048]{1,0:T(8,128)S(1)}, f32[8,2048]{1,0:T(8,128)S(1)}, u32[]{:S(2)}, u32[]{:S(2)}) collective-permute-start(f32[8,2048]{1,0:T(8,128)S(1)} %get-tuple-element.13.refs_10_), channel_id=1, source_target_pairs={{0,2},{1,3},{2,4},{3,5},{4,6},{5,7},{6,8},{7,9},{8,10},{9,11},{10,... | collective-permute-start | bytes 196616 | tf_op jit(solution)/shard_map/ppermute | solution.py:367
  76.6 7.1 %collective-permute-start.8 = (f32[8,2048]{1,0:T(8,128)S(1)}, f32[8,2048]{1,0:T(8,128)S(1)}, u32[]{:S(2)}, u32[]{:S(2)}) collective-permute-start(f32[8,2048]{1,0:T(8,128)S(1)} %get-tuple-element.13.refs_10_), channel_id=1, source_target_pairs={{0,1},{1,2},{2,3},{3,4},{4,5},{5,6},{6,7},{7,8},{8,9},{9,10},{10,1... | collective-permute-start | bytes 196616 | tf_op jit(solution)/shard_map/ppermute | solution.py:367
  76.6 7.1 %collective-permute-start.9 = (f32[8,2048]{1,0:T(8,128)S(1)}, f32[8,2048]{1,0:T(8,128)S(1)}, u32[]{:S(2)}, u32[]{:S(2)}) collective-permute-start(f32[8,2048]{1,0:T(8,128)S(1)} %get-tuple-element.13.refs_10_), channel_id=1, source_target_pairs={{0,15},{1,0},{2,1},{3,2},{4,3},{5,4},{6,5},{7,6},{8,7},{9,8},{10,9... | collective-permute-start | bytes 196616 | tf_op jit(solution)/shard_map/ppermute | solution.py:367
  81.0 4.8 %collective-permute-start.10 = (f32[8,2048]{1,0:T(8,128)S(1)}, f32[8,2048]{1,0:T(8,128)S(1)}, u32[]{:S(2)}, u32[]{:S(2)}) collective-permute-start(f32[8,2048]{1,0:T(8,128)S(1)} %get-tuple-element.13.refs_10_), channel_id=1, source_target_pairs={{0,14},{1,15},{2,0},{3,1},{4,2},{5,3},{6,4},{7,5},{8,6},{9,7},{10,... | collective-permute-start | bytes 196616 | tf_op jit(solution)/shard_map/ppermute | solution.py:367
  81.2 4.6 %collective-permute-start.11 = (f32[8,2048]{1,0:T(8,128)S(1)}, f32[8,2048]{1,0:T(8,128)S(1)}, u32[]{:S(2)}, u32[]{:S(2)}) collective-permute-start(f32[8,2048]{1,0:T(8,128)S(1)} %get-tuple-element.13.refs_10_), channel_id=1, source_target_pairs={{0,13},{1,14},{2,15},{3,0},{4,1},{5,2},{6,3},{7,4},{8,5},{9,6},{10... | collective-permute-start | bytes 196616 | tf_op jit(solution)/shard_map/ppermute | solution.py:367

commit v3 on v2

--- a/solution.py
+++ b/solution.py
@@ -11,10 +11,15 @@
 LANES = 128
 FIELDS = 16
 BINS = 128
-BATCH = 16
+GROUP = 4
+LARGEST = 8
+UNIT = 8
+RING = 4
+CACHED = 25
 TRANSPOSED = (((1,), (1,)), ((), ()))
 VMEM = pl.BlockSpec(memory_space=pltpu.VMEM)
 SMEM = pl.BlockSpec(memory_space=pltpu.SMEM)
+HBM = pl.BlockSpec(memory_space=pltpu.HBM)
 LIMIT = 40 * 2**20
 
 
@@ -229,73 +234,203 @@
         list_ref[r : r + 1, :] = row.astype(i32)
 
 
-def load_operands(hops, shares, vectors, where_scr, vec_scr):
+def load_where(hops, shares, where_scr):
     chunks = shares[0].shape[1] // LANES
     for nb in range(2 * hops + 1):
         for c in range(chunks):
-            lanes = slice(c * LANES, (c + 1) * LANES)
-            where_scr[nb * chunks + c] = shares[nb][8:16, lanes]
-            value = vectors[nb][0:8, lanes]
+            where_scr[nb * chunks + c] = shares[nb][8:16, c * LANES : (c + 1) * LANES]
+    where_scr[(2 * hops + 1) * chunks] = jnp.zeros((8, LANES), f32)
+
+
+def load_vectors(hops, vectors, vec_scr):
+    chunks = vectors[0].shape[1] // LANES
+    for nb in range(2 * hops + 1):
+        for c in range(chunks):
+            value = vectors[nb][0:8, c * LANES : (c + 1) * LANES]
             high = value.astype(bf16)
             low = (value - high.astype(f32)).astype(bf16)
             vec_scr[nb * chunks + c] = jnp.concatenate([high, low], axis=0)
-    last = (2 * hops + 1) * chunks
-    where_scr[last] = jnp.zeros((8, LANES), f32)
-    vec_scr[last] = jnp.zeros((16, LANES), bf16)
-
-
-def product(hops, list_smem, where_scr, vec_scr, out_ref):
+    vec_scr[(2 * hops + 1) * chunks] = jnp.zeros((16, LANES), bf16)
+
+
+def block(x_col, y_col, x_row, y_row):
+    dx = x_col - x_row
+    dy = y_col - y_row
+    square = jnp.maximum(dx * dx + dy * dy, 1e-30)
+    distance = square * lax.rsqrt(square)
+    inside = jnp.maximum(4.0 - distance, 0.0)
+    inside = inside * inside
+    corr = inside * inside * (distance + 1.0)
+    high = corr.astype(bf16)
+    return high, (corr - high.astype(f32)).astype(bf16)
+
+
+def group_blocks(list_smem, where_scr, vec_scr, r, start, columns):
+    highs, lows, vecs = [], [], []
+    for j in range(GROUP):
+        c = list_smem[r, start + j]
+        high, low = block(*columns, where_scr[c, 0:1, :], where_scr[c, 1:2, :])
+        highs.append(high)
+        lows.append(low)
+        vecs.append(vec_scr[c])
+    return highs, lows, vecs
+
+
+def multiply(total, highs, lows, vecs):
+    vec = jnp.concatenate(vecs, axis=1)
+    total = total + dot_t(vec, jnp.concatenate(highs, axis=1))
+    return total + dot_t(vec, jnp.concatenate(lows, axis=1))
+
+
+def groups_of(list_smem, r):
+    return (list_smem[r, LANES - 1] + (GROUP - 1)) // GROUP
+
+
+def own_columns(hops, chunks, where_scr, r):
+    column = where_scr[hops * chunks + r].T
+    return tuple(jnp.broadcast_to(column[:, k : k + 1], (LANES, LANES)) for k in range(2))
+
+
+def in_batches(count, batch):
+    total = lax.fori_loop(
+        0, count // LARGEST, lambda b, t: batch(b * LARGEST, LARGEST, t), jnp.zeros((16, LANES), f32)
+    )
+    size = LARGEST // 2
+    while size:
+        first = count // (2 * size) * (2 * size)
+        total = lax.cond(
+            (count // size) % 2 == 1,
+            lambda t, first=first, size=size: batch(first, size, t),
+            lambda t: t,
+            total,
+        )
+        size //= 2
+    return total
+
+
+def put_rows(out_ref, r, total):
+    out_ref[:, pl.ds(pl.multiple_of(r * LANES, LANES), LANES)] = total[0:8] + total[8:16]
+
+
+def first_touch(number, size):
+    return (number + size - 1) // UNIT != (number + UNIT - 1) // UNIT - 1
+
+
+def unit_of(stage, unit):
+    return stage.at[pl.ds((unit % RING) * UNIT, UNIT)]
+
+
+def product(hops, list_smem, where_scr, vec_scr, out_ref, cache_ref, stage, sems):
     chunks = out_ref.shape[1] // LANES
-
-    def chunk_rows(r, _):
-        column = where_scr[hops * chunks + r].T
-        x_col = jnp.broadcast_to(column[:, 0:1], (LANES, LANES))
-        y_col = jnp.broadcast_to(column[:, 1:2], (LANES, LANES))
-
-        def batch(start, size, total):
+    room = cache_ref.shape[0] - 1
+
+    def save(unit):
+        return pltpu.make_async_copy(
+            unit_of(stage, unit), cache_ref.at[jnp.minimum(unit, room)], sems.at[unit % RING]
+        )
+
+    def chunk_rows(r, before):
+        columns = own_columns(hops, chunks, where_scr, r)
+        count = groups_of(list_smem, r)
+
+        def batch(first, size, total):
+            number = before + first
+            touched = (number + size - 1) // UNIT
+            pl.when(first_touch(number, size) & (touched >= RING))(lambda: save(touched - RING).wait())
             highs, lows, vecs = [], [], []
-            for j in range(size):
-                c = list_smem[r, start + j]
-                dx = x_col - where_scr[c, 0:1, :]
-                dy = y_col - where_scr[c, 1:2, :]
-                square = jnp.maximum(dx * dx + dy * dy, 1e-30)
-                distance = square * lax.rsqrt(square)
-                inside = jnp.maximum(4.0 - distance, 0.0)
-                inside = inside * inside
-                corr = inside * inside * (distance + 1.0)
-                high = corr.astype(bf16)
-                highs.append(high)
-                lows.append((corr - high.astype(f32)).astype(bf16))
-                vecs.append(vec_scr[c])
-            vec = jnp.concatenate(vecs, axis=1)
-            total = total + dot_t(vec, jnp.concatenate(highs, axis=1))
-            return total + dot_t(vec, jnp.concatenate(lows, axis=1))
-
-        amount = list_smem[r, LANES - 1]
-        full = amount // BATCH
-        total = lax.fori_loop(
-            0, full, lambda b, t: batch(b * BATCH, BATCH, t), jnp.zeros((16, LANES), f32)
-        )
-        left = (amount - full * BATCH + 3) // 4
-        for size in range(4, BATCH + 1, 4):
-            total = lax.cond(
-                left == size // 4, lambda t, size=size: batch(full * BATCH, size, t), lambda t: t, total
+            for g in range(size):
+                high, low, vec = group_blocks(
+                    list_smem, where_scr, vec_scr, r, (first + g) * GROUP, columns
+                )
+                highs += high
+                lows += low
+                vecs += vec
+            for g in range(size):
+                slot = (number + g) % (RING * UNIT)
+                for j in range(GROUP):
+                    stage[slot, j] = highs[g * GROUP + j]
+                    stage[slot, GROUP + j] = lows[g * GROUP + j]
+            total = multiply(total, highs, lows, vecs)
+            full = number // UNIT
+            pl.when((number + size) // UNIT > full)(lambda: save(full).start())
+            return total
+
+        put_rows(out_ref, r, in_batches(count, batch))
+        return before + count
+
+    used = lax.fori_loop(0, chunks, chunk_rows, 0)
+    pl.when(used % UNIT != 0)(lambda: save(used // UNIT).start())
+    units = (used + UNIT - 1) // UNIT
+    for k in range(RING):
+        last = units - 1 - (units - 1 - k) % RING
+        pl.when(units > k)(lambda last=last: save(last).wait())
+
+
+def product_again(hops, list_smem, where_scr, vec_scr, out_ref, cache_ref, stage, sems, load):
+    chunks = out_ref.shape[1] // LANES
+    room = (cache_ref.shape[0] - 1) * UNIT
+
+    def sizes(r, state):
+        before, kept = state
+        after = before + groups_of(list_smem, r)
+        return after, jnp.where(after <= room, after, kept)
+
+    used, kept = lax.fori_loop(0, chunks, sizes, (0, 0))
+    units = (kept + UNIT - 1) // UNIT
+
+    def fetch(unit):
+        return pltpu.make_async_copy(cache_ref.at[unit], unit_of(stage, unit), sems.at[unit % RING])
+
+    for k in range(RING):
+        pl.when(k < units)(lambda k=k: fetch(k).start())
+    load(used > kept)
+
+    def chunk_rows(r, before):
+        count = groups_of(list_smem, r)
+
+        def kept_batch(first, size, total):
+            number = before + first
+            pl.when(first_touch(number, size))(lambda: fetch((number + size - 1) // UNIT).wait())
+            highs, lows, vecs = [], [], []
+            for g in range(size):
+                slot = (number + g) % (RING * UNIT)
+                for j in range(GROUP):
+                    highs.append(stage[slot, j])
+                    lows.append(stage[slot, GROUP + j])
+                    vecs.append(vec_scr[list_smem[r, (first + g) * GROUP + j]])
+            total = multiply(total, highs, lows, vecs)
+            full = number // UNIT
+            pl.when(((number + size) // UNIT > full) & (full + RING < units))(
+                lambda: fetch(full + RING).start()
             )
-        out_ref[:, pl.ds(pl.multiple_of(r * LANES, LANES), LANES)] = total[0:8] + total[8:16]
-        return 0
+            return total
+
+        def fresh(g, total):
+            columns = own_columns(hops, chunks, where_scr, r)
+            return multiply(total, *group_blocks(list_smem, where_scr, vec_scr, r, g * GROUP, columns))
+
+        total = lax.cond(
+            before + count <= kept,
+            lambda: in_batches(count, kept_batch),
+            lambda: lax.fori_loop(0, count, fresh, jnp.zeros((16, LANES), f32)),
+        )
+        put_rows(out_ref, r, total)
+        return before + count
 
     lax.fori_loop(0, chunks, chunk_rows, 0)
 
 
 def first_kernel(hops, tile_ref, own_ref, *refs):
     shares = refs[: 2 * hops + 1]
-    image_ref, share_ref, dots_ref, list_ref, list_smem, where_scr, vec_scr, sem = refs[2 * hops + 1 :]
+    image_ref, share_ref, dots_ref, list_ref, cache_ref = refs[2 * hops + 1 : 2 * hops + 6]
+    list_smem, where_scr, vec_scr, stage, sems, sem = refs[2 * hops + 6 :]
     make_list(hops, tile_ref, shares, list_ref)
     copy = pltpu.make_async_copy(list_ref, list_smem, sem)
     copy.start()
-    load_operands(hops, shares, shares, where_scr, vec_scr)
+    load_where(hops, shares, where_scr)
+    load_vectors(hops, shares, vec_scr)
     copy.wait()
-    product(hops, list_smem, where_scr, vec_scr, image_ref)
+    product(hops, list_smem, where_scr, vec_scr, image_ref, cache_ref, stage, sems)
     field = own_ref[4:12, :]
     image = own_ref[3:4, :] * field + own_ref[2:3, :] * image_ref[...]
     image_ref[...] = image
@@ -313,12 +448,16 @@
     dots_ref[...] = jnp.broadcast_to(dots[None], dots_ref.shape)
 
 
-def second_kernel(hops, list_smem, own_ref, image_ref, *refs):
+def second_kernel(hops, list_smem, own_ref, image_ref, cache_ref, *refs):
     n = 2 * hops + 1
     shares, vectors = refs[:n], refs[n : 2 * n]
-    twice_ref, where_scr, vec_scr = refs[2 * n :]
-    load_operands(hops, shares, vectors, where_scr, vec_scr)
-    product(hops, list_smem, where_scr, vec_scr, twice_ref)
+    twice_ref, where_scr, vec_scr, stage, sems = refs[2 * n :]
+
+    def load(needed):
+        load_vectors(hops, vectors, vec_scr)
+        pl.when(needed)(lambda: load_where(hops, shares, where_scr))
+
+    product_again(hops, list_smem, where_scr, vec_scr, twice_ref, cache_ref, stage, sems, load)
     twice_ref[...] = own_ref[3:4, :] * image_ref[...] + own_ref[2:3, :] * twice_ref[...]
 
 
@@ -353,7 +492,7 @@
         kernel,
         out_shape=[jax.ShapeDtypeStruct(shape, kind) for shape, kind in outs],
         in_specs=ins,
-        out_specs=[VMEM] * len(outs),
+        out_specs=[VMEM if len(shape) < 3 or kind != bf16 else HBM for shape, kind in outs],
         scratch_shapes=list(scratch),
         compiler_params=pltpu.CompilerParams(vmem_limit_bytes=limit),
     )
@@ -382,7 +521,7 @@
     (outbox,) = call(
         functools.partial(outbox_kernel, tiles, width),
         [((tiles, FIELDS, width), f32)],
-        [pl.BlockSpec(memory_space=pltpu.HBM)] * 5,
+        [HBM] * 5,
         [
             pltpu.VMEM((FIELDS, rows), f32),
             pltpu.VMEM((2, rows), f32),
@@ -403,10 +542,16 @@
         [pltpu.VMEM((chunks, LANES), i32)] * 2 + [pltpu.VMEM((boxes, BINS, LANES), f32)],
     )(inbox, pair_count)
     shares = around(share, hops, tiles)
-    operands = [pltpu.VMEM((held + 1, 8, LANES), f32), pltpu.VMEM((held + 1, 16, LANES), bf16)]
-    image, image_share, dots, near = call(
+    operands = [
+        pltpu.VMEM((held + 1, 8, LANES), f32),
+        pltpu.VMEM((held + 1, 16, LANES), bf16),
+        pltpu.VMEM((RING * UNIT, 2 * GROUP, LANES, LANES), bf16),
+        pltpu.SemaphoreType.DMA((RING,)),
+    ]
+    kept = (min(CACHED, held * chunks // (GROUP * UNIT)) + 1, UNIT, 2 * GROUP, LANES, LANES)
+    image, image_share, dots, near, cache = call(
         functools.partial(first_kernel, hops),
-        [((8, rows), f32), ((8, rows), f32), ((tiles, 8, LANES), f32), ((chunks, LANES), i32)],
+        [((8, rows), f32), ((8, rows), f32), ((tiles, 8, LANES), f32), ((chunks, LANES), i32), (kept, bf16)],
         [SMEM] + [VMEM] * (2 * hops + 2),
         [pltpu.SMEM((chunks, LANES), i32)] + operands + [pltpu.SemaphoreType.DMA],
     )(my_tile[None], own, *shares)
@@ -414,9 +559,9 @@
     (twice,) = call(
         functools.partial(second_kernel, hops),
         [((8, rows), f32)],
-        [SMEM] + [VMEM] * (4 * hops + 4),
+        [SMEM] + [VMEM] * 2 + [HBM] + [VMEM] * (4 * hops + 2),
         operands,
-    )(near, own, image, *shares, *vectors)
+    )(near, own, image, cache, *shares, *vectors)
 
     sums = jnp.sum(
         lax.all_to_all(dots, "tiles", split_axis=0, concat_axis=0, tiled=True), axis=0

time: 129 us -> 115 us (0.89); the launches traced: 127 us -> 116 us
  Pallas kernels: 46.6 us -> 36 us
  blocking collectives: 20.6 us -> 18 us
  starting transfers between devices: 35.6 us -> 37.6 us
    pallas_call x1, Pallas kernels: 18.4 us -> 9.39 us  [local(): call(functools.partial(second_kernel, hops), [((8, rows), f32)], [SMEM] +...]
    ppermute x12, starting transfers between devices: 16.2 us -> 24.6 us  [around(): got[sign * hop] = lax.ppermute(value, 'tiles', pairs)]
    all_to_all x1, starting transfers between devices: 11.9 us -> 5.68 us  [local(): lax.all_to_all(dots, 'tiles', split_axis=0, concat_axis=0, tiled=True)]
    all_to_all x1, blocking collectives: 20.6 us -> 18 us  [local(): lax.all_to_all(jnp.broadcast_to(parts[None], (tiles, 8, LANES)), 'tiles',...]
    pallas_call x1, Pallas kernels: 19.7 us -> 18.1 us  [local(): call(functools.partial(first_kernel, hops), [((8, rows), f32), ((8, rows)...]
  transfers between devices with their start and end apart: 14 -> 14, of which waited for: 6 -> 6; matrix products, arithmetic and copies ran while one was open for 0% -> 0% of each run, Pallas kernels for 14% -> 8%
where the time goes in v3:
time: 115 us; the launch traced here: 116 us
  starting transfers between devices  37.6 us (33%)
  Pallas kernels  36 us (31%)
  waiting for transfers between devices  22.3 us (19%)
  blocking collectives  18 us (16%)
  between operations  1.35 us (1%)
    ppermute x12, starting transfers between devices, around(): got[sign * hop] = lax.ppermute(value, 'tiles', pairs)  24.6 us
    pallas_call x1, Pallas kernels, local(): call(functools.partial(first_kernel, hops), [((8, rows), f32), ((8, rows)...  18.1 us
    all_to_all x1, blocking collectives, local(): lax.all_to_all(jnp.broadcast_to(parts[None], (tiles, 8, LANES)), 'tiles',...  18 us
    ppermute x12, waiting for transfers between devices, around(): got[sign * hop] = lax.ppermute(value, 'tiles', pairs)  12.9 us
    all_to_all x1, waiting for transfers between devices, local(): lax.all_to_all(outbox, 'tiles', split_axis=0, concat_axis=0, tiled=True)  9.4 us
    pallas_call x1, Pallas kernels, local(): call(functools.partial(second_kernel, hops), [((8, rows), f32)], [SMEM] +...  9.39 us
    all_to_all x1, starting transfers between devices, local(): lax.all_to_all(outbox, 'tiles', split_axis=0, concat_axis=0, tiled=True)  7.4 us
    all_to_all x1, starting transfers between devices, local(): lax.all_to_all(dots, 'tiles', split_axis=0, concat_axis=0, tiled=True)  5.68 us
  transfers between devices with their start and end apart: 14, of which 6 were waited for; matrix products, arithmetic and copies ran while one was open for 0% of the time, Pallas kernels for 8%

profile of v3, /device:TPU:0, one launch (start us, length us, event | category | flops | bytes accessed | tf_op | source)
XLA Modules:
  0.0 116.2 jit_solution(10899475691231708525)
XLA Ops:
  0.6 3.4 %shard_map.77 = f32[16,16,256]{2,1,0:T(8,128)} custom-call(f32[2,2048]{1,0:T(2,128)} %pos_ref.1, f32[1,2048]{1,0:T(1,128)} %bitcast.4, f32[1,2048]{1,0:T(1,128)} %bitcast.5, f32[8,2048]{1,0:T(8,128)} %innov_ref.1, s32[1,2048]{1,0:T(1,128)} %bitcast.6), custom_call_target="tpu_custom_call" | custom-call | tf_op jit(solution)/shard_map/pallas_call | solution.py:521
  4.0 7.4 %all-to-all-start = ((f32[16,16,256]{2,1,0:T(8,128)}), f32[16,16,256]{2,1,0:T(8,128)S(1)}, u32[]{:S(2)}, u32[]{:S(2)}) async-start(f32[16,16,256]{2,1,0:T(8,128)} %shard_map.77), calls=%async_computation | async-start | bytes 524288 | tf_op jit(solution)/shard_map/all_to_all | solution.py:537
  12.1 9.4 %all-to-all-done.in_ref = f32[16,16,256]{2,1,0:T(8,128)S(1)} async-done(((f32[16,16,256]{2,1,0:T(8,128)}), f32[16,16,256]{2,1,0:T(8,128)S(1)}, u32[]{:S(2)}, u32[]{:S(2)}) %all-to-all-start) | async-done | bytes 262176 | tf_op jit(solution)/shard_map/all_to_all | solution.py:537
  21.5 3.5 %shard_map.78 = (f32[16,2048]{1,0:T(8,128)S(1)}, f32[16,2048]{1,0:T(8,128)S(1)}) custom-call(f32[16,16,256]{2,1,0:T(8,128)S(1)} %all-to-all-done.in_ref, s32[1]{0:T(128)S(6)} %copy.8.count_ref), custom_call_target="tpu_custom_call" | custom-call | tf_op jit(solution)/shard_map/pallas_call | solution.py:538
  25.0 0.2 collective-permute-start
  25.2 1.6 %collective-permute-start.1 = (f32[16,2048]{1,0:T(8,128)S(1)}, f32[16,2048]{1,0:T(8,128)S(1)}, u32[]{:S(2)}, u32[]{:S(2)}) collective-permute-start(f32[16,2048]{1,0:T(8,128)S(1)} %get-tuple-element.10.refs_3_), channel_id=1, source_target_pairs={{0,2},{1,3},{2,4},{3,5},{4,6},{5,7},{6,8},{7,9},{8,10},{9,11},{10,... | collective-permute-start | bytes 393224 | tf_op jit(solution)/shard_map/ppermute | solution.py:506
  26.8 0.0 collective-permute-start.2
  26.8 4.4 %collective-permute-start.3 = (f32[16,2048]{1,0:T(8,128)S(1)}, f32[16,2048]{1,0:T(8,128)S(1)}, u32[]{:S(2)}, u32[]{:S(2)}) collective-permute-start(f32[16,2048]{1,0:T(8,128)S(1)} %get-tuple-element.10.refs_3_), channel_id=1, source_target_pairs={{0,15},{1,0},{2,1},{3,2},{4,3},{5,4},{6,5},{7,6},{8,7},{9,8},{10,9... | collective-permute-start | bytes 393224 | tf_op jit(solution)/shard_map/ppermute | solution.py:506
  31.3 0.4 collective-permute-start.4
  31.7 0.0 collective-permute-done.refs_0_
  31.7 0.5 collective-permute-start.5
  32.2 5.1 %collective-permute-done.1.refs_1_ = f32[16,2048]{1,0:T(8,128)S(1)} collective-permute-done((f32[16,2048]{1,0:T(8,128)S(1)}, f32[16,2048]{1,0:T(8,128)S(1)}, u32[]{:S(2)}, u32[]{:S(2)}) %collective-permute-start.1) | collective-permute-done | bytes 131104 | tf_op jit(solution)/shard_map/ppermute | solution.py:506
  37.3 0.0 collective-permute-done.2.refs_2_
  37.3 0.0 collective-permute-done.3.refs_4_
  37.3 4.2 %collective-permute-done.4.refs_5_ = f32[16,2048]{1,0:T(8,128)S(1)} collective-permute-done((f32[16,2048]{1,0:T(8,128)S(1)}, f32[16,2048]{1,0:T(8,128)S(1)}, u32[]{:S(2)}, u32[]{:S(2)}) %collective-permute-start.4) | collective-permute-done | bytes 131104 | tf_op jit(solution)/shard_map/ppermute | solution.py:506
  41.5 0.0 collective-permute-done.5.refs_6_
  41.5 18.1 %shard_map.79 = (f32[8,2048]{1,0:T(8,128)S(1)}, f32[8,2048]{1,0:T(8,128)S(1)}, f32[16,8,128]{2,1,0:T(8,128)}, s32[16,128]{1,0:T(8,128)S(1)}, bf16[26,8,8,128,128]{4,3,2,1,0:T(8,128)(2,1)}) custom-call(s32[1]{0:T(128)} %bitcast.3.tile_ref, f32[16,2048]{1,0:T(8,128)S(1)} %get-tuple-element.9.own_ref, f32[16,2048]{1,0:T(8,128)S(1)} %collective-permute-done.refs_0_, ...), custom_call_target="tpu_custom_call" | custom-call | tf_op jit(solution)/shard_map/pallas_call | solution.py:552
  59.7 9.8 %collective-permute-start.6 = (f32[8,2048]{1,0:T(8,128)S(1)}, f32[8,2048]{1,0:T(8,128)S(1)}, u32[]{:S(2)}, u32[]{:S(2)}) collective-permute-start(f32[8,2048]{1,0:T(8,128)S(1)} %get-tuple-element.15.refs_10_), channel_id=1, source_target_pairs={{0,3},{1,4},{2,5},{3,6},{4,7},{5,8},{6,9},{7,10},{8,11},{9,12},{10... | collective-permute-start | bytes 196616 | tf_op jit(solution)/shard_map/ppermute | solution.py:506
  69.5 5.7 %all-to-all-start.1 = ((f32[16,8,128]{2,1,0:T(8,128)}), f32[16,8,128]{2,1,0:T(8,128)S(1)}, u32[]{:S(2)}, u32[]{:S(2)}) async-start(f32[16,8,128]{2,1,0:T(8,128)} %get-tuple-element.11), calls=%async_computation.1 | async-start | bytes 131072 | tf_op jit(solution)/shard_map/all_to_all | solution.py:567
  75.1 1.9 %collective-permute-start.7 = (f32[8,2048]{1,0:T(8,128)S(1)}, f32[8,2048]{1,0:T(8,128)S(1)}, u32[]{:S(2)}, u32[]{:S(2)}) collective-permute-start(f32[8,2048]{1,0:T(8,128)S(1)} %get-tuple-element.15.refs_10_), channel_id=1, source_target_pairs={{0,2},{1,3},{2,4},{3,5},{4,6},{5,7},{6,8},{7,9},{8,10},{9,11},{10,... | collective-permute-start | bytes 196616 | tf_op jit(solution)/shard_map/ppermute | solution.py:506
  77.1 0.3 collective-permute-start.8
  77.3 4.2 %collective-permute-start.9 = (f32[8,2048]{1,0:T(8,128)S(1)}, f32[8,2048]{1,0:T(8,128)S(1)}, u32[]{:S(2)}, u32[]{:S(2)}) collective-permute-start(f32[8,2048]{1,0:T(8,128)S(1)} %get-tuple-element.15.refs_10_), channel_id=1, source_target_pairs={{0,15},{1,0},{2,1},{3,2},{4,3},{5,4},{6,5},{7,6},{8,7},{9,8},{10,9... | collective-permute-start | bytes 196616 | tf_op jit(solution)/shard_map/ppermute | solution.py:506
  81.5 0.2 collective-permute-start.10
  81.7 0.0 collective-permute-done.6.refs_7_
  81.7 1.1 collective-permute-start.11
  82.8 1.2 %collective-permute-done.7.refs_8_ = f32[8,2048]{1,0:T(8,128)S(1)} collective-permute-done((f32[8,2048]{1,0:T(8,128)S(1)}, f32[8,2048]{1,0:T(8,128)S(1)}, u32[]{:S(2)}, u32[]{:S(2)}) %collective-permute-start.7) | collective-permute-done | bytes 65568 | tf_op jit(solution)/shard_map/ppermute | solution.py:506
  84.0 0.2 collective-permute-done.8.refs_9_
  84.2 0.0 collective-permute-done.9.refs_11_
  84.2 2.1 %collective-permute-done.10.refs_12_ = f32[8,2048]{1,0:T(8,128)S(1)} collective-permute-done((f32[8,2048]{1,0:T(8,128)S(1)}, f32[8,2048]{1,0:T(8,128)S(1)}, u32[]{:S(2)}, u32[]{:S(2)}) %collective-permute-start.10) | collective-permute-done | bytes 65568 | tf_op jit(solution)/shard_map/ppermute | solution.py:506
  86.3 0.0 collective-permute-done.11.refs_13_
  86.3 9.4 %shard_map.80 = f32[8,2048]{1,0:T(8,128)S(1)} custom-call(s32[16,128]{1,0:T(8,128)S(1)} %get-tuple-element.13.list_smem, f32[16,2048]{1,0:T(8,128)S(1)} %get-tuple-element.9.own_ref, f32[8,2048]{1,0:T(8,128)S(1)} %get-tuple-element.12.image_ref, bf16[26,8,8,128,128]{4,3,2,1,0:T(8,128)(2,1)} %get-tuple-element.14.cache_ref, ...), custom_call_target="tpu_custom_call" | custom-call | tf_op jit(solution)/shard_map/pallas_call | solution.py:559
  95.7 0.0 all-to-all-done.1
  95.8 0.2 subtract_divide_fusion
  95.9 0.1 add_reduce_fusion
  96.1 0.2 multiply_reduce_fusion.1
  96.3 0.2 multiply_reduce_fusion
  96.5 0.1 broadcast_select_fusion
  96.6 18.0 %all_to_all.15.both_ref = f32[16,8,128]{2,1,0:T(8,128)S(1)} all-to-all(f32[16,8,128]{2,1,0:T(8,128)S(1)} %broadcast_in_dim.57), channel_id=1, replica_groups=mesh['groups'=2,'tiles'=16] {'tiles'}, dimensions={0} | all-to-all | bytes 131072 | tf_op jit(solution)/shard_map/all_to_all | solution.py:581
  114.6 0.1 broadcast_in_dim.58.alpha_ref
  114.7 1.6 %shard_map.81 = (f32[8,2048]{1,0:T(8,128)}, f32[8,2048]{1,0:T(8,128)}) custom-call(f32[16,2048]{1,0:T(8,128)S(1)} %get-tuple-element.9.own_ref, f32[16,8,128]{2,1,0:T(8,128)S(1)} %all_to_all.15.both_ref, f32[8,128]{1,0:T(8,128)S(1)} %broadcast_in_dim.58.alpha_ref, f32[8,2048]{1,0:T(8,128)S(1)} %get-tuple-element.22.direction_ref, ...), custom_call_target="tpu_custom_call" | custom-call | tf_op jit(solution)/shard_map/pallas_call | solution.py:585
  (3 shorter events, 0.0 us)
Async XLA Ops:
  4.0 17.5 %all-to-all-start = ((f32[16,16,256]{2,1,0:T(8,128)}), f32[16,16,256]{2,1,0:T(8,128)S(1)}, u32[]{:S(2)}, u32[]{:S(2)}) async-start(f32[16,16,256]{2,1,0:T(8,128)} %shard_map.77), calls=%async_computation | async-start | bytes 524288 | tf_op jit(solution)/shard_map/all_to_all | solution.py:537
  25.0 6.7 %collective-permute-start = (f32[16,2048]{1,0:T(8,128)S(1)}, f32[16,2048]{1,0:T(8,128)S(1)}, u32[]{:S(2)}, u32[]{:S(2)}) collective-permute-start(f32[16,2048]{1,0:T(8,128)S(1)} %get-tuple-element.10.refs_3_), channel_id=1, source_target_pairs={{0,3},{1,4},{2,5},{3,6},{4,7},{5,8},{6,9},{7,10},{8,11},{9,12},{10... | collective-permute-start | bytes 393224 | tf_op jit(solution)/shard_map/ppermute | solution.py:506
  25.2 12.2 %collective-permute-start.1 = (f32[16,2048]{1,0:T(8,128)S(1)}, f32[16,2048]{1,0:T(8,128)S(1)}, u32[]{:S(2)}, u32[]{:S(2)}) collective-permute-start(f32[16,2048]{1,0:T(8,128)S(1)} %get-tuple-element.10.refs_3_), channel_id=1, source_target_pairs={{0,2},{1,3},{2,4},{3,5},{4,6},{5,7},{6,8},{7,9},{8,10},{9,11},{10,... | collective-permute-start | bytes 393224 | tf_op jit(solution)/shard_map/ppermute | solution.py:506
  26.8 10.5 %collective-permute-start.2 = (f32[16,2048]{1,0:T(8,128)S(1)}, f32[16,2048]{1,0:T(8,128)S(1)}, u32[]{:S(2)}, u32[]{:S(2)}) collective-permute-start(f32[16,2048]{1,0:T(8,128)S(1)} %get-tuple-element.10.refs_3_), channel_id=1, source_target_pairs={{0,1},{1,2},{2,3},{3,4},{4,5},{5,6},{6,7},{7,8},{8,9},{9,10},{10,1... | collective-permute-start | bytes 393224 | tf_op jit(solution)/shard_map/ppermute | solution.py:506
  26.8 10.5 %collective-permute-start.3 = (f32[16,2048]{1,0:T(8,128)S(1)}, f32[16,2048]{1,0:T(8,128)S(1)}, u32[]{:S(2)}, u32[]{:S(2)}) collective-permute-start(f32[16,2048]{1,0:T(8,128)S(1)} %get-tuple-element.10.refs_3_), channel_id=1, source_target_pairs={{0,15},{1,0},{2,1},{3,2},{4,3},{5,4},{6,5},{7,6},{8,7},{9,8},{10,9... | collective-permute-start | bytes 393224 | tf_op jit(solution)/shard_map/ppermute | solution.py:506
  31.3 10.3 %collective-permute-start.4 = (f32[16,2048]{1,0:T(8,128)S(1)}, f32[16,2048]{1,0:T(8,128)S(1)}, u32[]{:S(2)}, u32[]{:S(2)}) collective-permute-start(f32[16,2048]{1,0:T(8,128)S(1)} %get-tuple-element.10.refs_3_), channel_id=1, source_target_pairs={{0,14},{1,15},{2,0},{3,1},{4,2},{5,3},{6,4},{7,5},{8,6},{9,7},{10,... | collective-permute-start | bytes 393224 | tf_op jit(solution)/shard_map/ppermute | solution.py:506
  31.7 9.9 %collective-permute-start.5 = (f32[16,2048]{1,0:T(8,128)S(1)}, f32[16,2048]{1,0:T(8,128)S(1)}, u32[]{:S(2)}, u32[]{:S(2)}) collective-permute-start(f32[16,2048]{1,0:T(8,128)S(1)} %get-tuple-element.10.refs_3_), channel_id=1, source_target_pairs={{0,13},{1,14},{2,15},{3,0},{4,1},{5,2},{6,3},{7,4},{8,5},{9,6},{10... | collective-permute-start | bytes 393224 | tf_op jit(solution)/shard_map/ppermute | solution.py:506
  59.7 22.0 %collective-permute-start.6 = (f32[8,2048]{1,0:T(8,128)S(1)}, f32[8,2048]{1,0:T(8,128)S(1)}, u32[]{:S(2)}, u32[]{:S(2)}) collective-permute-start(f32[8,2048]{1,0:T(8,128)S(1)} %get-tuple-element.15.refs_10_), channel_id=1, source_target_pairs={{0,3},{1,4},{2,5},{3,6},{4,7},{5,8},{6,9},{7,10},{8,11},{9,12},{10... | collective-permute-start | bytes 196616 | tf_op jit(solution)/shard_map/ppermute | solution.py:506
  69.5 26.3 %all-to-all-start.1 = ((f32[16,8,128]{2,1,0:T(8,128)}), f32[16,8,128]{2,1,0:T(8,128)S(1)}, u32[]{:S(2)}, u32[]{:S(2)}) async-start(f32[16,8,128]{2,1,0:T(8,128)} %get-tuple-element.11), calls=%async_computation.1 | async-start | bytes 131072 | tf_op jit(solution)/shard_map/all_to_all | solution.py:567
  75.1 8.8 %collective-permute-start.7 = (f32[8,2048]{1,0:T(8,128)S(1)}, f32[8,2048]{1,0:T(8,128)S(1)}, u32[]{:S(2)}, u32[]{:S(2)}) collective-permute-start(f32[8,2048]{1,0:T(8,128)S(1)} %get-tuple-element.15.refs_10_), channel_id=1, source_target_pairs={{0,2},{1,3},{2,4},{3,5},{4,6},{5,7},{6,8},{7,9},{8,10},{9,11},{10,... | collective-permute-start | bytes 196616 | tf_op jit(solution)/shard_map/ppermute | solution.py:506
  77.1 7.1 %collective-permute-start.8 = (f32[8,2048]{1,0:T(8,128)S(1)}, f32[8,2048]{1,0:T(8,128)S(1)}, u32[]{:S(2)}, u32[]{:S(2)}) collective-permute-start(f32[8,2048]{1,0:T(8,128)S(1)} %get-tuple-element.15.refs_10_), channel_id=1, source_target_pairs={{0,1},{1,2},{2,3},{3,4},{4,5},{5,6},{6,7},{7,8},{8,9},{9,10},{10,1... | collective-permute-start | bytes 196616 | tf_op jit(solution)/shard_map/ppermute | solution.py:506
  77.3 6.9 %collective-permute-start.9 = (f32[8,2048]{1,0:T(8,128)S(1)}, f32[8,2048]{1,0:T(8,128)S(1)}, u32[]{:S(2)}, u32[]{:S(2)}) collective-permute-start(f32[8,2048]{1,0:T(8,128)S(1)} %get-tuple-element.15.refs_10_), channel_id=1, source_target_pairs={{0,15},{1,0},{2,1},{3,2},{4,3},{5,4},{6,5},{7,6},{8,7},{9,8},{10,9... | collective-permute-start | bytes 196616 | tf_op jit(solution)/shard_map/ppermute | solution.py:506
  81.5 4.8 %collective-permute-start.10 = (f32[8,2048]{1,0:T(8,128)S(1)}, f32[8,2048]{1,0:T(8,128)S(1)}, u32[]{:S(2)}, u32[]{:S(2)}) collective-permute-start(f32[8,2048]{1,0:T(8,128)S(1)} %get-tuple-element.15.refs_10_), channel_id=1, source_target_pairs={{0,14},{1,15},{2,0},{3,1},{4,2},{5,3},{6,4},{7,5},{8,6},{9,7},{10,... | collective-permute-start | bytes 196616 | tf_op jit(solution)/shard_map/ppermute | solution.py:506
  81.7 4.6 %collective-permute-start.11 = (f32[8,2048]{1,0:T(8,128)S(1)}, f32[8,2048]{1,0:T(8,128)S(1)}, u32[]{:S(2)}, u32[]{:S(2)}) collective-permute-start(f32[8,2048]{1,0:T(8,128)S(1)} %get-tuple-element.15.refs_10_), channel_id=1, source_target_pairs={{0,13},{1,14},{2,15},{3,0},{4,1},{5,2},{6,3},{7,4},{8,5},{9,6},{10... | collective-permute-start | bytes 196616 | tf_op jit(solution)/shard_map/ppermute | solution.py:506

commit v4 on v2

--- a/solution.py
+++ b/solution.py
@@ -11,10 +11,14 @@
 LANES = 128
 FIELDS = 16
 BINS = 128
-BATCH = 16
+GROUP = 4
+UNIT = 8
+RING = 4
+CACHED = 25
 TRANSPOSED = (((1,), (1,)), ((), ()))
 VMEM = pl.BlockSpec(memory_space=pltpu.VMEM)
 SMEM = pl.BlockSpec(memory_space=pltpu.SMEM)
+HBM = pl.BlockSpec(memory_space=pltpu.HBM)
 LIMIT = 40 * 2**20
 
 
@@ -229,73 +233,175 @@
         list_ref[r : r + 1, :] = row.astype(i32)
 
 
-def load_operands(hops, shares, vectors, where_scr, vec_scr):
+def load_where(hops, shares, where_scr):
     chunks = shares[0].shape[1] // LANES
     for nb in range(2 * hops + 1):
         for c in range(chunks):
-            lanes = slice(c * LANES, (c + 1) * LANES)
-            where_scr[nb * chunks + c] = shares[nb][8:16, lanes]
-            value = vectors[nb][0:8, lanes]
+            where_scr[nb * chunks + c] = shares[nb][8:16, c * LANES : (c + 1) * LANES]
+    where_scr[(2 * hops + 1) * chunks] = jnp.zeros((8, LANES), f32)
+
+
+def load_vectors(hops, vectors, vec_scr):
+    chunks = vectors[0].shape[1] // LANES
+    for nb in range(2 * hops + 1):
+        for c in range(chunks):
+            value = vectors[nb][0:8, c * LANES : (c + 1) * LANES]
             high = value.astype(bf16)
             low = (value - high.astype(f32)).astype(bf16)
             vec_scr[nb * chunks + c] = jnp.concatenate([high, low], axis=0)
-    last = (2 * hops + 1) * chunks
-    where_scr[last] = jnp.zeros((8, LANES), f32)
-    vec_scr[last] = jnp.zeros((16, LANES), bf16)
-
-
-def product(hops, list_smem, where_scr, vec_scr, out_ref):
-    chunks = out_ref.shape[1] // LANES
-
-    def chunk_rows(r, _):
+    vec_scr[(2 * hops + 1) * chunks] = jnp.zeros((16, LANES), bf16)
+
+
+def block(x_col, y_col, x_row, y_row):
+    dx = x_col - x_row
+    dy = y_col - y_row
+    square = jnp.maximum(dx * dx + dy * dy, 1e-30)
+    distance = square * lax.rsqrt(square)
+    inside = jnp.maximum(4.0 - distance, 0.0)
+    inside = inside * inside
+    corr = inside * inside * (distance + 1.0)
+    high = corr.astype(bf16)
+    return high, (corr - high.astype(f32)).astype(bf16)
+
+
+def multiply(total, high, low, vec):
+    both = jnp.concatenate([high, low], axis=1)
+    return total + dot_t(jnp.concatenate([vec, vec], axis=1), both)
+
+
+def flatten(list_smem, flat, chunks):
+    def chunk_rows(r, number):
+        def one(g, number):
+            flat[number] = r * LANES + g * GROUP
+            return number + 1
+
+        return lax.fori_loop(0, (list_smem[r, LANES - 1] + (GROUP - 1)) // GROUP, one, number)
+
+    number = lax.fori_loop(0, chunks, chunk_rows, 0)
+    for k in range(UNIT):
+        flat[number + k] = LANES - 2 * GROUP
+    return (number + UNIT - 1) // UNIT
+
+
+def own_columns(hops, chunks, where_scr, columns):
+    for r in range(chunks):
         column = where_scr[hops * chunks + r].T
-        x_col = jnp.broadcast_to(column[:, 0:1], (LANES, LANES))
-        y_col = jnp.broadcast_to(column[:, 1:2], (LANES, LANES))
-
-        def batch(start, size, total):
-            highs, lows, vecs = [], [], []
-            for j in range(size):
-                c = list_smem[r, start + j]
-                dx = x_col - where_scr[c, 0:1, :]
-                dy = y_col - where_scr[c, 1:2, :]
-                square = jnp.maximum(dx * dx + dy * dy, 1e-30)
-                distance = square * lax.rsqrt(square)
-                inside = jnp.maximum(4.0 - distance, 0.0)
-                inside = inside * inside
-                corr = inside * inside * (distance + 1.0)
-                high = corr.astype(bf16)
-                highs.append(high)
-                lows.append((corr - high.astype(f32)).astype(bf16))
-                vecs.append(vec_scr[c])
-            vec = jnp.concatenate(vecs, axis=1)
-            total = total + dot_t(vec, jnp.concatenate(highs, axis=1))
-            return total + dot_t(vec, jnp.concatenate(lows, axis=1))
-
-        amount = list_smem[r, LANES - 1]
-        full = amount // BATCH
-        total = lax.fori_loop(
-            0, full, lambda b, t: batch(b * BATCH, BATCH, t), jnp.zeros((16, LANES), f32)
+        for k in range(2):
+            columns[k, r] = jnp.broadcast_to(column[:, k : k + 1], (LANES, LANES))
+
+
+def ring_slot(stage, unit):
+    return stage.at[unit % RING]
+
+
+def group(list_smem, where_scr, vec_scr, columns, entry, total, keep):
+    r, start = entry // LANES, entry % LANES
+    x_col, y_col = columns[0, r], columns[1, r]
+    for j in range(GROUP):
+        c = list_smem[r, start + j]
+        high, low = block(x_col, y_col, where_scr[c, 0:1, :], where_scr[c, 1:2, :])
+        total = multiply(total, high, low, vec_scr[c])
+        keep.append((high, low))
+    return total
+
+
+def add_rows(sums, entry, total):
+    r = entry // LANES
+    sums[r] = sums[r] + (total[0:8] + total[8:16])
+
+
+def put_rows(out_ref, sums):
+    for r in range(sums.shape[0]):
+        out_ref[:, r * LANES : (r + 1) * LANES] = sums[r]
+
+
+def product(list_smem, flat, where_scr, vec_scr, columns, sums, cache_ref, stage, sems):
+    room = cache_ref.shape[0] - 1
+    blank = jnp.zeros((16, LANES), f32)
+    sums[...] = jnp.zeros_like(sums)
+    units = flatten(list_smem, flat, sums.shape[0])
+
+    def save(unit):
+        return pltpu.make_async_copy(
+            ring_slot(stage, unit), cache_ref.at[jnp.minimum(unit, room)], sems.at[unit % RING]
         )
-        left = (amount - full * BATCH + 3) // 4
-        for size in range(4, BATCH + 1, 4):
-            total = lax.cond(
-                left == size // 4, lambda t, size=size: batch(full * BATCH, size, t), lambda t: t, total
-            )
-        out_ref[:, pl.ds(pl.multiple_of(r * LANES, LANES), LANES)] = total[0:8] + total[8:16]
+
+    def one_unit(unit, _):
+        pl.when(unit >= RING)(lambda: save(unit - RING).wait())
+        slot = unit % RING
+        entries = [flat[unit * UNIT + g] for g in range(UNIT)]
+        kept, totals = [], []
+        for entry in entries:
+            totals.append(group(list_smem, where_scr, vec_scr, columns, entry, blank, kept))
+        for k, (high, low) in enumerate(kept):
+            stage[slot, 2 * k] = high
+            stage[slot, 2 * k + 1] = low
+        for entry, total in zip(entries, totals):
+            add_rows(sums, entry, total)
+        save(unit).start()
         return 0
 
-    lax.fori_loop(0, chunks, chunk_rows, 0)
+    lax.fori_loop(0, units, one_unit, 0)
+    for k in range(RING):
+        last = units - 1 - (units - 1 - k) % RING
+        pl.when(units > k)(lambda last=last: save(last).wait())
+
+
+def product_again(list_smem, flat, where_scr, vec_scr, columns, sums, cache_ref, stage, sems, load):
+    room = cache_ref.shape[0] - 1
+    blank = jnp.zeros((16, LANES), f32)
+    sums[...] = jnp.zeros_like(sums)
+    units = flatten(list_smem, flat, sums.shape[0])
+    ready = jnp.minimum(units, room)
+
+    def fetch(unit):
+        return pltpu.make_async_copy(cache_ref.at[unit], ring_slot(stage, unit), sems.at[unit % RING])
+
+    for k in range(RING):
+        pl.when(k < ready)(lambda k=k: fetch(k).start())
+    load(units > ready)
+
+    def one_unit(unit, _):
+        fetch(unit).wait()
+        slot = unit % RING
+        entries = [flat[unit * UNIT + g] for g in range(UNIT)]
+        totals = []
+        for g, entry in enumerate(entries):
+            r, start = entry // LANES, entry % LANES
+            total = blank
+            for j in range(GROUP):
+                k = g * GROUP + j
+                vec = vec_scr[list_smem[r, start + j]]
+                total = multiply(total, stage[slot, 2 * k], stage[slot, 2 * k + 1], vec)
+            totals.append(total)
+        for entry, total in zip(entries, totals):
+            add_rows(sums, entry, total)
+        pl.when(unit + RING < ready)(lambda: fetch(unit + RING).start())
+        return 0
+
+    lax.fori_loop(0, ready, one_unit, 0)
+
+    def fresh(number, _):
+        entry = flat[number]
+        add_rows(sums, entry, group(list_smem, where_scr, vec_scr, columns, entry, blank, []))
+        return 0
+
+    lax.fori_loop(ready * UNIT, units * UNIT, fresh, 0)
 
 
 def first_kernel(hops, tile_ref, own_ref, *refs):
     shares = refs[: 2 * hops + 1]
-    image_ref, share_ref, dots_ref, list_ref, list_smem, where_scr, vec_scr, sem = refs[2 * hops + 1 :]
+    image_ref, share_ref, dots_ref, list_ref, cache_ref = refs[2 * hops + 1 : 2 * hops + 6]
+    list_smem, flat, where_scr, vec_scr, columns, sums, stage, sems, sem = refs[2 * hops + 6 :]
     make_list(hops, tile_ref, shares, list_ref)
     copy = pltpu.make_async_copy(list_ref, list_smem, sem)
     copy.start()
-    load_operands(hops, shares, shares, where_scr, vec_scr)
+    load_where(hops, shares, where_scr)
+    load_vectors(hops, shares, vec_scr)
+    own_columns(hops, own_ref.shape[1] // LANES, where_scr, columns)
     copy.wait()
-    product(hops, list_smem, where_scr, vec_scr, image_ref)
+    product(list_smem, flat, where_scr, vec_scr, columns, sums, cache_ref, stage, sems)
+    put_rows(image_ref, sums)
     field = own_ref[4:12, :]
     image = own_ref[3:4, :] * field + own_ref[2:3, :] * image_ref[...]
     image_ref[...] = image
@@ -313,12 +419,22 @@
     dots_ref[...] = jnp.broadcast_to(dots[None], dots_ref.shape)
 
 
-def second_kernel(hops, list_smem, own_ref, image_ref, *refs):
+def second_kernel(hops, list_smem, own_ref, image_ref, cache_ref, *refs):
     n = 2 * hops + 1
     shares, vectors = refs[:n], refs[n : 2 * n]
-    twice_ref, where_scr, vec_scr = refs[2 * n :]
-    load_operands(hops, shares, vectors, where_scr, vec_scr)
-    product(hops, list_smem, where_scr, vec_scr, twice_ref)
+    twice_ref, flat, where_scr, vec_scr, columns, sums, stage, sems = refs[2 * n :]
+
+    def load(needed):
+        load_vectors(hops, vectors, vec_scr)
+
+
+        @pl.when(needed)
+        def _():
+            load_where(hops, shares, where_scr)
+            own_columns(hops, own_ref.shape[1] // LANES, where_scr, columns)
+
+    product_again(list_smem, flat, where_scr, vec_scr, columns, sums, cache_ref, stage, sems, load)
+    put_rows(twice_ref, sums)
     twice_ref[...] = own_ref[3:4, :] * image_ref[...] + own_ref[2:3, :] * twice_ref[...]
 
 
@@ -353,7 +469,7 @@
         kernel,
         out_shape=[jax.ShapeDtypeStruct(shape, kind) for shape, kind in outs],
         in_specs=ins,
-        out_specs=[VMEM] * len(outs),
+        out_specs=[VMEM if len(shape) < 3 or kind != bf16 else HBM for shape, kind in outs],
         scratch_shapes=list(scratch),
         compiler_params=pltpu.CompilerParams(vmem_limit_bytes=limit),
     )
@@ -382,7 +498,7 @@
     (outbox,) = call(
         functools.partial(outbox_kernel, tiles, width),
         [((tiles, FIELDS, width), f32)],
-        [pl.BlockSpec(memory_space=pltpu.HBM)] * 5,
+        [HBM] * 5,
         [
             pltpu.VMEM((FIELDS, rows), f32),
             pltpu.VMEM((2, rows), f32),
@@ -403,10 +519,19 @@
         [pltpu.VMEM((chunks, LANES), i32)] * 2 + [pltpu.VMEM((boxes, BINS, LANES), f32)],
     )(inbox, pair_count)
     shares = around(share, hops, tiles)
-    operands = [pltpu.VMEM((held + 1, 8, LANES), f32), pltpu.VMEM((held + 1, 16, LANES), bf16)]
-    image, image_share, dots, near = call(
+    operands = [
+        pltpu.SMEM((held * chunks // GROUP + UNIT,), i32),
+        pltpu.VMEM((held + 1, 8, LANES), f32),
+        pltpu.VMEM((held + 1, 16, LANES), bf16),
+        pltpu.VMEM((2, chunks, LANES, LANES), f32),
+        pltpu.VMEM((chunks, 8, LANES), f32),
+        pltpu.VMEM((RING, UNIT * 2 * GROUP, LANES, LANES), bf16),
+        pltpu.SemaphoreType.DMA((RING,)),
+    ]
+    kept = (min(CACHED, held * chunks // (GROUP * UNIT)) + 1, UNIT * 2 * GROUP, LANES, LANES)
+    image, image_share, dots, near, cache = call(
         functools.partial(first_kernel, hops),
-        [((8, rows), f32), ((8, rows), f32), ((tiles, 8, LANES), f32), ((chunks, LANES), i32)],
+        [((8, rows), f32), ((8, rows), f32), ((tiles, 8, LANES), f32), ((chunks, LANES), i32), (kept, bf16)],
         [SMEM] + [VMEM] * (2 * hops + 2),
         [pltpu.SMEM((chunks, LANES), i32)] + operands + [pltpu.SemaphoreType.DMA],
     )(my_tile[None], own, *shares)
@@ -414,9 +539,9 @@
     (twice,) = call(
         functools.partial(second_kernel, hops),
         [((8, rows), f32)],
-        [SMEM] + [VMEM] * (4 * hops + 4),
+        [SMEM] + [VMEM] * 2 + [HBM] + [VMEM] * (4 * hops + 2),
         operands,
-    )(near, own, image, *shares, *vectors)
+    )(near, own, image, cache, *shares, *vectors)
 
     sums = jnp.sum(
         lax.all_to_all(dots, "tiles", split_axis=0, concat_axis=0, tiled=True), axis=0

time: 129 us -> 109 us (0.84)
  Pallas kernels: 46.6 us -> 33.7 us
  blocking collectives: 20.6 us -> 15 us
    pallas_call x1, Pallas kernels: 18.4 us -> 9.14 us  [local(): call(functools.partial(second_kernel, hops), [((8, rows), f32)], [SMEM] +...]
    all_to_all x1, blocking collectives: 20.6 us -> 15 us  [local(): lax.all_to_all(jnp.broadcast_to(parts[None], (tiles, 8, LANES)), 'tiles',...]
    pallas_call x1, Pallas kernels: 19.7 us -> 16.1 us  [local(): call(functools.partial(first_kernel, hops), [((8, rows), f32), ((8, rows)...]
    all_to_all x1, starting transfers between devices: 11.9 us -> 9.79 us  [local(): lax.all_to_all(dots, 'tiles', split_axis=0, concat_axis=0, tiled=True)]
    ppermute x12, starting transfers between devices: 16.2 us -> 17.9 us  [around(): got[sign * hop] = lax.ppermute(value, 'tiles', pairs)]
  transfers between devices with their start and end apart: 14 -> 14, of which waited for: 6 -> 6; matrix products, arithmetic and copies ran while one was open for 0% -> 0% of each run, Pallas kernels for 14% -> 8%
where the time goes in v4:
time: 109 us; the launch traced here: 108 us
  starting transfers between devices  35.1 us (32%)
  Pallas kernels  33.7 us (31%)
  waiting for transfers between devices  22.3 us (20%)
  blocking collectives  15 us (14%)
  between operations  1.35 us (1%)
    ppermute x12, starting transfers between devices, around(): got[sign * hop] = lax.ppermute(value, 'tiles', pairs)  17.9 us
    pallas_call x1, Pallas kernels, local(): call(functools.partial(first_kernel, hops), [((8, rows), f32), ((8, rows)...  16.1 us
    all_to_all x1, blocking collectives, local(): lax.all_to_all(jnp.broadcast_to(parts[None], (tiles, 8, LANES)), 'tiles',...  15 us
    ppermute x12, waiting for transfers between devices, around(): got[sign * hop] = lax.ppermute(value, 'tiles', pairs)  12.9 us
    all_to_all x1, starting transfers between devices, local(): lax.all_to_all(dots, 'tiles', split_axis=0, concat_axis=0, tiled=True)  9.79 us
    all_to_all x1, waiting for transfers between devices, local(): lax.all_to_all(outbox, 'tiles', split_axis=0, concat_axis=0, tiled=True)  9.4 us
    pallas_call x1, Pallas kernels, local(): call(functools.partial(second_kernel, hops), [((8, rows), f32)], [SMEM] +...  9.14 us
    all_to_all x1, starting transfers between devices, local(): lax.all_to_all(outbox, 'tiles', split_axis=0, concat_axis=0, tiled=True)  7.4 us
  transfers between devices with their start and end apart: 14, of which 6 were waited for; matrix products, arithmetic and copies ran while one was open for 0% of the time, Pallas kernels for 8%

profile of v4, /device:TPU:0, one launch (start us, length us, event | category | flops | bytes accessed | tf_op | source)
XLA Modules:
  0.0 108.4 jit_solution(13211374499109500261)
XLA Ops:
  0.6 3.4 %shard_map.77 = f32[16,16,256]{2,1,0:T(8,128)} custom-call(f32[2,2048]{1,0:T(2,128)} %pos_ref.1, f32[1,2048]{1,0:T(1,128)} %bitcast.4, f32[1,2048]{1,0:T(1,128)} %bitcast.5, f32[8,2048]{1,0:T(8,128)} %innov_ref.1, s32[1,2048]{1,0:T(1,128)} %bitcast.6), custom_call_target="tpu_custom_call" | custom-call | tf_op jit(solution)/shard_map/pallas_call | solution.py:498
  4.0 7.4 %all-to-all-start = ((f32[16,16,256]{2,1,0:T(8,128)}), f32[16,16,256]{2,1,0:T(8,128)S(1)}, u32[]{:S(2)}, u32[]{:S(2)}) async-start(f32[16,16,256]{2,1,0:T(8,128)} %shard_map.77), calls=%async_computation | async-start | bytes 524288 | tf_op jit(solution)/shard_map/all_to_all | solution.py:514
  12.1 9.4 %all-to-all-done.in_ref = f32[16,16,256]{2,1,0:T(8,128)S(1)} async-done(((f32[16,16,256]{2,1,0:T(8,128)}), f32[16,16,256]{2,1,0:T(8,128)S(1)}, u32[]{:S(2)}, u32[]{:S(2)}) %all-to-all-start) | async-done | bytes 262176 | tf_op jit(solution)/shard_map/all_to_all | solution.py:514
  21.5 3.5 %shard_map.78 = (f32[16,2048]{1,0:T(8,128)S(1)}, f32[16,2048]{1,0:T(8,128)S(1)}) custom-call(f32[16,16,256]{2,1,0:T(8,128)S(1)} %all-to-all-done.in_ref, s32[1]{0:T(128)S(6)} %copy.8.count_ref), custom_call_target="tpu_custom_call" | custom-call | tf_op jit(solution)/shard_map/pallas_call | solution.py:515
  25.0 0.2 collective-permute-start
  25.2 1.6 %collective-permute-start.1 = (f32[16,2048]{1,0:T(8,128)S(1)}, f32[16,2048]{1,0:T(8,128)S(1)}, u32[]{:S(2)}, u32[]{:S(2)}) collective-permute-start(f32[16,2048]{1,0:T(8,128)S(1)} %get-tuple-element.10.refs_3_), channel_id=1, source_target_pairs={{0,2},{1,3},{2,4},{3,5},{4,6},{5,7},{6,8},{7,9},{8,10},{9,11},{10,... | collective-permute-start | bytes 393224 | tf_op jit(solution)/shard_map/ppermute | solution.py:483
  26.8 0.0 collective-permute-start.2
  26.8 4.4 %collective-permute-start.3 = (f32[16,2048]{1,0:T(8,128)S(1)}, f32[16,2048]{1,0:T(8,128)S(1)}, u32[]{:S(2)}, u32[]{:S(2)}) collective-permute-start(f32[16,2048]{1,0:T(8,128)S(1)} %get-tuple-element.10.refs_3_), channel_id=1, source_target_pairs={{0,15},{1,0},{2,1},{3,2},{4,3},{5,4},{6,5},{7,6},{8,7},{9,8},{10,9... | collective-permute-start | bytes 393224 | tf_op jit(solution)/shard_map/ppermute | solution.py:483
  31.3 0.4 collective-permute-start.4
  31.7 0.0 collective-permute-done.refs_0_
  31.7 0.5 collective-permute-start.5
  32.2 5.1 %collective-permute-done.1.refs_1_ = f32[16,2048]{1,0:T(8,128)S(1)} collective-permute-done((f32[16,2048]{1,0:T(8,128)S(1)}, f32[16,2048]{1,0:T(8,128)S(1)}, u32[]{:S(2)}, u32[]{:S(2)}) %collective-permute-start.1) | collective-permute-done | bytes 131104 | tf_op jit(solution)/shard_map/ppermute | solution.py:483
  37.3 0.0 collective-permute-done.2.refs_2_
  37.3 0.0 collective-permute-done.3.refs_4_
  37.3 4.2 %collective-permute-done.4.refs_5_ = f32[16,2048]{1,0:T(8,128)S(1)} collective-permute-done((f32[16,2048]{1,0:T(8,128)S(1)}, f32[16,2048]{1,0:T(8,128)S(1)}, u32[]{:S(2)}, u32[]{:S(2)}) %collective-permute-start.4) | collective-permute-done | bytes 131104 | tf_op jit(solution)/shard_map/ppermute | solution.py:483
  41.5 0.0 collective-permute-done.5.refs_6_
  41.5 16.1 %shard_map.79 = (f32[8,2048]{1,0:T(8,128)S(1)}, f32[8,2048]{1,0:T(8,128)S(1)}, f32[16,8,128]{2,1,0:T(8,128)}, s32[16,128]{1,0:T(8,128)S(1)}, bf16[26,64,128,128]{3,2,1,0:T(8,128)(2,1)}) custom-call(s32[1]{0:T(128)} %bitcast.3.tile_ref, f32[16,2048]{1,0:T(8,128)S(1)} %get-tuple-element.9.own_ref, f32[16,2048]{1,0:T(8,128)S(1)} %collective-permute-done.refs_0_, ...), custom_call_target="tpu_custom_call" | custom-call | tf_op jit(solution)/shard_map/pallas_call | solution.py:532
  57.6 3.1 %collective-permute-start.6 = (f32[8,2048]{1,0:T(8,128)S(1)}, f32[8,2048]{1,0:T(8,128)S(1)}, u32[]{:S(2)}, u32[]{:S(2)}) collective-permute-start(f32[8,2048]{1,0:T(8,128)S(1)} %get-tuple-element.15.refs_10_), channel_id=1, source_target_pairs={{0,3},{1,4},{2,5},{3,6},{4,7},{5,8},{6,9},{7,10},{8,11},{9,12},{10... | collective-permute-start | bytes 196616 | tf_op jit(solution)/shard_map/ppermute | solution.py:483
  60.7 9.8 %all-to-all-start.1 = ((f32[16,8,128]{2,1,0:T(8,128)}), f32[16,8,128]{2,1,0:T(8,128)S(1)}, u32[]{:S(2)}, u32[]{:S(2)}) async-start(f32[16,8,128]{2,1,0:T(8,128)} %get-tuple-element.11), calls=%async_computation.1 | async-start | bytes 131072 | tf_op jit(solution)/shard_map/all_to_all | solution.py:547
  70.5 1.9 %collective-permute-start.7 = (f32[8,2048]{1,0:T(8,128)S(1)}, f32[8,2048]{1,0:T(8,128)S(1)}, u32[]{:S(2)}, u32[]{:S(2)}) collective-permute-start(f32[8,2048]{1,0:T(8,128)S(1)} %get-tuple-element.15.refs_10_), channel_id=1, source_target_pairs={{0,2},{1,3},{2,4},{3,5},{4,6},{5,7},{6,8},{7,9},{8,10},{9,11},{10,... | collective-permute-start | bytes 196616 | tf_op jit(solution)/shard_map/ppermute | solution.py:483
  72.5 0.0 collective-permute-start.8
  72.5 4.4 %collective-permute-start.9 = (f32[8,2048]{1,0:T(8,128)S(1)}, f32[8,2048]{1,0:T(8,128)S(1)}, u32[]{:S(2)}, u32[]{:S(2)}) collective-permute-start(f32[8,2048]{1,0:T(8,128)S(1)} %get-tuple-element.15.refs_10_), channel_id=1, source_target_pairs={{0,15},{1,0},{2,1},{3,2},{4,3},{5,4},{6,5},{7,6},{8,7},{9,8},{10,9... | collective-permute-start | bytes 196616 | tf_op jit(solution)/shard_map/ppermute | solution.py:483
  76.9 0.2 collective-permute-start.10
  77.1 0.0 collective-permute-done.6.refs_7_
  77.1 1.1 collective-permute-start.11
  78.1 1.2 %collective-permute-done.7.refs_8_ = f32[8,2048]{1,0:T(8,128)S(1)} collective-permute-done((f32[8,2048]{1,0:T(8,128)S(1)}, f32[8,2048]{1,0:T(8,128)S(1)}, u32[]{:S(2)}, u32[]{:S(2)}) %collective-permute-start.7) | collective-permute-done | bytes 65568 | tf_op jit(solution)/shard_map/ppermute | solution.py:483
  79.3 0.2 collective-permute-done.8.refs_9_
  79.6 0.0 collective-permute-done.9.refs_11_
  79.6 2.1 %collective-permute-done.10.refs_12_ = f32[8,2048]{1,0:T(8,128)S(1)} collective-permute-done((f32[8,2048]{1,0:T(8,128)S(1)}, f32[8,2048]{1,0:T(8,128)S(1)}, u32[]{:S(2)}, u32[]{:S(2)}) %collective-permute-start.10) | collective-permute-done | bytes 65568 | tf_op jit(solution)/shard_map/ppermute | solution.py:483
  81.7 0.0 collective-permute-done.11.refs_13_
  81.7 9.1 %shard_map.80 = f32[8,2048]{1,0:T(8,128)S(1)} custom-call(s32[16,128]{1,0:T(8,128)S(1)} %get-tuple-element.13.list_smem, f32[16,2048]{1,0:T(8,128)S(1)} %get-tuple-element.9.own_ref, f32[8,2048]{1,0:T(8,128)S(1)} %get-tuple-element.12.image_ref, bf16[26,64,128,128]{3,2,1,0:T(8,128)(2,1)} %get-tuple-element.14.cache_ref, ...), custom_call_target="tpu_custom_call" | custom-call | tf_op jit(solution)/shard_map/pallas_call | solution.py:539
  90.9 0.0 all-to-all-done.1
  90.9 0.2 subtract_divide_fusion
  91.1 0.1 add_reduce_fusion
  91.2 0.2 multiply_reduce_fusion.1
  91.4 0.2 multiply_reduce_fusion
  91.6 0.1 broadcast_select_fusion
  91.7 15.0 %all_to_all.15.both_ref = f32[16,8,128]{2,1,0:T(8,128)S(1)} all-to-all(f32[16,8,128]{2,1,0:T(8,128)S(1)} %broadcast_in_dim.57), channel_id=1, replica_groups=mesh['groups'=2,'tiles'=16] {'tiles'}, dimensions={0} | all-to-all | bytes 131072 | tf_op jit(solution)/shard_map/all_to_all | solution.py:561
  106.7 0.1 broadcast_in_dim.58.alpha_ref
  106.8 1.6 %shard_map.81 = (f32[8,2048]{1,0:T(8,128)}, f32[8,2048]{1,0:T(8,128)}) custom-call(f32[16,2048]{1,0:T(8,128)S(1)} %get-tuple-element.9.own_ref, f32[16,8,128]{2,1,0:T(8,128)S(1)} %all_to_all.15.both_ref, f32[8,128]{1,0:T(8,128)S(1)} %broadcast_in_dim.58.alpha_ref, f32[8,2048]{1,0:T(8,128)S(1)} %get-tuple-element.22.direction_ref, ...), custom_call_target="tpu_custom_call" | custom-call | tf_op jit(solution)/shard_map/pallas_call | solution.py:565
  (3 shorter events, 0.0 us)
Async XLA Ops:
  4.0 17.5 %all-to-all-start = ((f32[16,16,256]{2,1,0:T(8,128)}), f32[16,16,256]{2,1,0:T(8,128)S(1)}, u32[]{:S(2)}, u32[]{:S(2)}) async-start(f32[16,16,256]{2,1,0:T(8,128)} %shard_map.77), calls=%async_computation | async-start | bytes 524288 | tf_op jit(solution)/shard_map/all_to_all | solution.py:514
  25.0 6.7 %collective-permute-start = (f32[16,2048]{1,0:T(8,128)S(1)}, f32[16,2048]{1,0:T(8,128)S(1)}, u32[]{:S(2)}, u32[]{:S(2)}) collective-permute-start(f32[16,2048]{1,0:T(8,128)S(1)} %get-tuple-element.10.refs_3_), channel_id=1, source_target_pairs={{0,3},{1,4},{2,5},{3,6},{4,7},{5,8},{6,9},{7,10},{8,11},{9,12},{10... | collective-permute-start | bytes 393224 | tf_op jit(solution)/shard_map/ppermute | solution.py:483
  25.2 12.2 %collective-permute-start.1 = (f32[16,2048]{1,0:T(8,128)S(1)}, f32[16,2048]{1,0:T(8,128)S(1)}, u32[]{:S(2)}, u32[]{:S(2)}) collective-permute-start(f32[16,2048]{1,0:T(8,128)S(1)} %get-tuple-element.10.refs_3_), channel_id=1, source_target_pairs={{0,2},{1,3},{2,4},{3,5},{4,6},{5,7},{6,8},{7,9},{8,10},{9,11},{10,... | collective-permute-start | bytes 393224 | tf_op jit(solution)/shard_map/ppermute | solution.py:483
  26.8 10.5 %collective-permute-start.2 = (f32[16,2048]{1,0:T(8,128)S(1)}, f32[16,2048]{1,0:T(8,128)S(1)}, u32[]{:S(2)}, u32[]{:S(2)}) collective-permute-start(f32[16,2048]{1,0:T(8,128)S(1)} %get-tuple-element.10.refs_3_), channel_id=1, source_target_pairs={{0,1},{1,2},{2,3},{3,4},{4,5},{5,6},{6,7},{7,8},{8,9},{9,10},{10,1... | collective-permute-start | bytes 393224 | tf_op jit(solution)/shard_map/ppermute | solution.py:483
  26.8 10.5 %collective-permute-start.3 = (f32[16,2048]{1,0:T(8,128)S(1)}, f32[16,2048]{1,0:T(8,128)S(1)}, u32[]{:S(2)}, u32[]{:S(2)}) collective-permute-start(f32[16,2048]{1,0:T(8,128)S(1)} %get-tuple-element.10.refs_3_), channel_id=1, source_target_pairs={{0,15},{1,0},{2,1},{3,2},{4,3},{5,4},{6,5},{7,6},{8,7},{9,8},{10,9... | collective-permute-start | bytes 393224 | tf_op jit(solution)/shard_map/ppermute | solution.py:483
  31.3 10.3 %collective-permute-start.4 = (f32[16,2048]{1,0:T(8,128)S(1)}, f32[16,2048]{1,0:T(8,128)S(1)}, u32[]{:S(2)}, u32[]{:S(2)}) collective-permute-start(f32[16,2048]{1,0:T(8,128)S(1)} %get-tuple-element.10.refs_3_), channel_id=1, source_target_pairs={{0,14},{1,15},{2,0},{3,1},{4,2},{5,3},{6,4},{7,5},{8,6},{9,7},{10,... | collective-permute-start | bytes 393224 | tf_op jit(solution)/shard_map/ppermute | solution.py:483
  31.7 9.9 %collective-permute-start.5 = (f32[16,2048]{1,0:T(8,128)S(1)}, f32[16,2048]{1,0:T(8,128)S(1)}, u32[]{:S(2)}, u32[]{:S(2)}) collective-permute-start(f32[16,2048]{1,0:T(8,128)S(1)} %get-tuple-element.10.refs_3_), channel_id=1, source_target_pairs={{0,13},{1,14},{2,15},{3,0},{4,1},{5,2},{6,3},{7,4},{8,5},{9,6},{10... | collective-permute-start | bytes 393224 | tf_op jit(solution)/shard_map/ppermute | solution.py:483
  57.6 19.4 %collective-permute-start.6 = (f32[8,2048]{1,0:T(8,128)S(1)}, f32[8,2048]{1,0:T(8,128)S(1)}, u32[]{:S(2)}, u32[]{:S(2)}) collective-permute-start(f32[8,2048]{1,0:T(8,128)S(1)} %get-tuple-element.15.refs_10_), channel_id=1, source_target_pairs={{0,3},{1,4},{2,5},{3,6},{4,7},{5,8},{6,9},{7,10},{8,11},{9,12},{10... | collective-permute-start | bytes 196616 | tf_op jit(solution)/shard_map/ppermute | solution.py:483
  60.7 30.1 %all-to-all-start.1 = ((f32[16,8,128]{2,1,0:T(8,128)}), f32[16,8,128]{2,1,0:T(8,128)S(1)}, u32[]{:S(2)}, u32[]{:S(2)}) async-start(f32[16,8,128]{2,1,0:T(8,128)} %get-tuple-element.11), calls=%async_computation.1 | async-start | bytes 131072 | tf_op jit(solution)/shard_map/all_to_all | solution.py:547
  70.5 8.8 %collective-permute-start.7 = (f32[8,2048]{1,0:T(8,128)S(1)}, f32[8,2048]{1,0:T(8,128)S(1)}, u32[]{:S(2)}, u32[]{:S(2)}) collective-permute-start(f32[8,2048]{1,0:T(8,128)S(1)} %get-tuple-element.15.refs_10_), channel_id=1, source_target_pairs={{0,2},{1,3},{2,4},{3,5},{4,6},{5,7},{6,8},{7,9},{8,10},{9,11},{10,... | collective-permute-start | bytes 196616 | tf_op jit(solution)/shard_map/ppermute | solution.py:483
  72.5 7.1 %collective-permute-start.8 = (f32[8,2048]{1,0:T(8,128)S(1)}, f32[8,2048]{1,0:T(8,128)S(1)}, u32[]{:S(2)}, u32[]{:S(2)}) collective-permute-start(f32[8,2048]{1,0:T(8,128)S(1)} %get-tuple-element.15.refs_10_), channel_id=1, source_target_pairs={{0,1},{1,2},{2,3},{3,4},{4,5},{5,6},{6,7},{7,8},{8,9},{9,10},{10,1... | collective-permute-start | bytes 196616 | tf_op jit(solution)/shard_map/ppermute | solution.py:483
  72.5 7.1 %collective-permute-start.9 = (f32[8,2048]{1,0:T(8,128)S(1)}, f32[8,2048]{1,0:T(8,128)S(1)}, u32[]{:S(2)}, u32[]{:S(2)}) collective-permute-start(f32[8,2048]{1,0:T(8,128)S(1)} %get-tuple-element.15.refs_10_), channel_id=1, source_target_pairs={{0,15},{1,0},{2,1},{3,2},{4,3},{5,4},{6,5},{7,6},{8,7},{9,8},{10,9... | collective-permute-start | bytes 196616 | tf_op jit(solution)/shard_map/ppermute | solution.py:483
  76.9 4.8 %collective-permute-start.10 = (f32[8,2048]{1,0:T(8,128)S(1)}, f32[8,2048]{1,0:T(8,128)S(1)}, u32[]{:S(2)}, u32[]{:S(2)}) collective-permute-start(f32[8,2048]{1,0:T(8,128)S(1)} %get-tuple-element.15.refs_10_), channel_id=1, source_target_pairs={{0,14},{1,15},{2,0},{3,1},{4,2},{5,3},{6,4},{7,5},{8,6},{9,7},{10,... | collective-permute-start | bytes 196616 | tf_op jit(solution)/shard_map/ppermute | solution.py:483
  77.1 4.6 %collective-permute-start.11 = (f32[8,2048]{1,0:T(8,128)S(1)}, f32[8,2048]{1,0:T(8,128)S(1)}, u32[]{:S(2)}, u32[]{:S(2)}) collective-permute-start(f32[8,2048]{1,0:T(8,128)S(1)} %get-tuple-element.15.refs_10_), channel_id=1, source_target_pairs={{0,13},{1,14},{2,15},{3,0},{4,1},{5,2},{6,3},{7,4},{8,5},{9,6},{10... | collective-permute-start | bytes 196616 | tf_op jit(solution)/shard_map/ppermute | solution.py:483
